TPU v7x, 512 devices: a whole 4x4x16 slice. The times are simulated.
512 devices in a mesh: group: 32 (over z_hi, x, core), tp: 16 (over z_lo, y).
Axes of the slice: x: 4, y: 4, z: 16 (z_hi: 4, z_lo: 4; z = z_hi * 4 + z_lo), core: 2. Of those that a mesh axis runs over, the one named last changes fastest.
Arguments:
- queries: bfloat16 [512, 4096], P('group', 'tp'), may hold values from -45 to 45
- new_key: bfloat16 [512, 4, 128], P('group'), may hold values from -12 to 12
- new_value: bfloat16 [512, 4, 128], P('group'), may hold values from -6 to 6
- lengths: int32 [512], P('group'), may hold values from 1 to 16384, as said below
- slot_row: int32 [32, 64], P('group'), may hold values from 0 to 15
- slot_block: int32 [32, 64], P('group'), may hold values from 0 to 32, as said below
- key_cache: bfloat16 [32, 64, 16, 128, 128], P('group', None, 'tp'), may hold values from -12 to 12
- value_cache: bfloat16 [32, 64, 16, 128, 128], P('group', None, 'tp'), may hold values from -6 to 6
Outputs:
- attended: bfloat16 [512, 4096], P('group', 'tp')
Inputs may be any that keep to these rules, and one draw needn't show every extreme that they name: `lengths`: the largest length is 16384, reached in every group. A rollout of n cached tokens has its blocks 0 to ceil(n / 512) - 1 each in exactly one slot with owner its group, on any group; every other slot holds block index 32. `slot_block`: empty slots hold 32.
All inputs are finite; a program needn't handle non-finite values.
Results may differ from a plain program's by a relative error of at most 0.0021.
Values may be sent and summed in bfloat16 or wider, within the bound.
A program may use at most 64 MiB of HBM per device.

v0:
```python
import jax
import jax.numpy as jnp
from jax import lax
from jax.sharding import PartitionSpec as P

QH = 32
KVH = 4
HD = 128
BLK = 512


def block_partials(
    slot_queries, slot_lengths, blocks, keys_here, values_here, share, sub_len, score_scale
):
    scores = (
        jnp.einsum("kgd,kpd->kgp", slot_queries, keys_here, preferred_element_type=jnp.float32)
        * score_scale
    )
    places = blocks[:, None] * BLK + share * sub_len + jnp.arange(sub_len, dtype=jnp.int32)[None, :]
    valid = (places < slot_lengths[:, None])[:, None, :]
    masked = jnp.where(valid, scores, -1e30)
    block_max = jnp.max(masked, axis=2)
    probs = jnp.where(valid, jnp.exp(masked - block_max[..., None]), 0.0)
    block_sum = jnp.sum(probs, axis=2)
    block_out = jnp.einsum(
        "kgp,kpd->kgd", probs.astype(jnp.bfloat16), values_here, preferred_element_type=jnp.float32
    )
    return (block_max, block_sum, block_out)


def gather_rows(member, block_max):
    return jnp.max(jnp.where(member[:, :, None], block_max[:, None, :], -1e30), axis=0)


def on_device(queries, new_key, new_value, lengths, slot_row, slot_block, key_cache, value_cache):
    seq_per = queries.shape[0]
    helpers = lax.axis_size("group")
    slot_count = slot_row.shape[1]
    per_pair = slot_count // helpers
    group_heads = QH // KVH
    sub_len = key_cache.shape[3]
    score_scale = HD ** (-0.5)
    tp_place = lax.axis_index("tp")
    kv_head = tp_place % KVH
    share = tp_place // KVH
    group_place = lax.axis_index("group")
    all_heads = lax.all_gather(queries, "tp", axis=1, tiled=True)
    own_queries = lax.dynamic_slice_in_dim(
        all_heads, kv_head * group_heads * HD, group_heads * HD, 1
    ).reshape(seq_per, group_heads, HD)
    keys_here = key_cache[0, :, 0]
    values_here = value_cache[0, :, 0]
    rows_local = slot_row[0]
    blocks = slot_block[0]
    every_query, every_length = (
        lax.all_gather(own_queries, "group", axis=0, tiled=True),
        lax.all_gather(lengths, "group", axis=0, tiled=True),
    )
    seq_total = every_query.shape[0]
    owners = jnp.arange(slot_count, dtype=jnp.int32) // per_pair
    seq_rows = owners * seq_per + rows_local
    block_max, block_sum, block_out = block_partials(
        every_query[seq_rows],
        every_length[seq_rows],
        blocks,
        keys_here,
        values_here,
        share,
        sub_len,
        score_scale,
    )
    member = seq_rows[:, None] == jnp.arange(seq_total, dtype=jnp.int32)[None, :]
    local_top = gather_rows(member, block_max)
    global_top = lax.pmax(local_top, "group")
    weights = jnp.exp(block_max - global_top[seq_rows])
    one_hot = member.astype(jnp.float32).T
    numer = jnp.dot(
        one_hot,
        (block_out * weights[..., None]).reshape(slot_count, group_heads * HD),
        precision=lax.Precision.HIGHEST,
    )
    denom = jnp.dot(one_hot, block_sum * weights, precision=lax.Precision.HIGHEST)
    numer_own, denom_own = (
        lax.psum_scatter(numer, "group", scatter_dimension=0, tiled=True),
        lax.psum_scatter(denom, "group", scatter_dimension=0, tiled=True),
    )
    top_own = lax.dynamic_slice_in_dim(global_top, group_place * seq_per, seq_per, 0)
    fresh_key = lax.dynamic_index_in_dim(new_key, kv_head, 1, keepdims=False)
    fresh_value = lax.dynamic_index_in_dim(new_value, kv_head, 1, keepdims=False).astype(
        jnp.float32
    )
    new_score = (
        jnp.einsum("sgd,sd->sg", own_queries, fresh_key, preferred_element_type=jnp.float32)
        * score_scale
    )
    is_first = share == 0
    candidate = jnp.where(is_first, new_score, -1e30)
    device_top = jnp.maximum(top_own, candidate)
    keep_factor = jnp.exp(top_own - device_top)
    fresh_factor = jnp.where(is_first, jnp.exp(candidate - device_top), 0.0)
    numer_dev = (
        numer_own.reshape(seq_per, group_heads, HD) * keep_factor[..., None]
        + fresh_factor[..., None] * fresh_value[:, None, :]
    )
    denom_dev = denom_own * keep_factor + fresh_factor
    wide_top = lax.dynamic_update_slice_in_dim(
        jnp.full((seq_per, QH), -1e30, jnp.float32), device_top, kv_head * group_heads, 1
    )
    head_top = lax.pmax(wide_top, "tp")
    mine_top = lax.dynamic_slice_in_dim(head_top, kv_head * group_heads, group_heads, 1)
    rescale = jnp.exp(device_top - mine_top)
    wide_numer = lax.dynamic_update_slice_in_dim(
        jnp.zeros((seq_per, QH * HD), jnp.float32),
        (numer_dev * rescale[..., None]).reshape(seq_per, group_heads * HD),
        kv_head * group_heads * HD,
        1,
    )
    wide_denom = lax.dynamic_update_slice_in_dim(
        jnp.zeros((seq_per, QH), jnp.float32), denom_dev * rescale, kv_head * group_heads, 1
    )
    part_numer, part_denom = (
        lax.psum_scatter(wide_numer, "tp", scatter_dimension=1, tiled=True),
        lax.psum_scatter(wide_denom, "tp", scatter_dimension=1, tiled=True),
    )
    heads_here = part_denom.shape[1]
    result = part_numer.reshape(seq_per, heads_here, HD) / part_denom[..., None]
    return result.reshape(seq_per, heads_here * HD).astype(jnp.bfloat16)


def solution(mesh):
    in_specs = (
        P("group", "tp"),
        P("group", None, None),
        P("group", None, None),
        P("group"),
        P("group", None),
        P("group", None),
        P("group", None, "tp", None, None),
        P("group", None, "tp", None, None),
    )
    out_specs = P("group", "tp")
    return jax.shard_map(
        on_device, mesh=mesh, in_specs=in_specs, out_specs=out_specs, check_vma=False
    )
```

profile of v0, /device:TPU:6, one launch (start us, length us, event | category | flops | bytes accessed | tf_op | source)
XLA Modules:
  0.0 620.5 jit_solution(10657982004035186813)
XLA Ops:
  6.5 0.0 copy-start
  6.5 0.0 all-gather.2.cloned.1.call-start
  6.5 44.8 %all_gather.10 = bf16[16,4096]{1,0:T(8,128)(2,1)S(1)} all-gather(bf16[16,256]{1,0:T(8,128)(2,1)} %param.8), channel_id=1, replica_groups=mesh['group'=32,'tp'=16] {'tp'}, dimensions={1}, use_global_device_ids=true | all-gather | bytes 139264 | tf_op jit(solution)/shard_map/all_gather | solution.py:47
  51.4 0.6 copy.31
  52.0 0.0 all-gather.2.cloned.1.call-update
  52.0 0.0 reduce-scatter.11.cloned.1.call-start
  52.1 1.3 dynamic-slice
  54.0 0.9 dynamic-update-slice
  54.9 24.0 %all-reduce = s32[512]{0:T(512)S(1)} all-reduce(s32[512]{0:T(512)S(1)} %dynamic-update-slice), channel_id=1, replica_groups=mesh['group'=32,'tp'=16] {'group'}, use_global_device_ids=true, to_apply=%add | all-reduce | flops 512 | bytes 4096
  78.8 0.7 fusion.34
  79.5 0.8 gather_fusion
  80.3 0.7 fusion.31
  81.0 0.7 add_bitcast_fusion
  81.6 0.1 add_compare_fusion
  81.7 0.1 iota_compare_fusion
  81.8 39.2 %all-gather.2.cloned.1.call-done = bf16[512,8,128]{2,1,0:T(8,128)(2,1)} async-done(((bf16[16,8,128]{2,1,0:T(8,128)(2,1)}), bf16[512,8,128]{2,1,0:T(8,128)(2,1)}) %all-gather.2.cloned.1.call-update) | async-done | bytes 1048592 | tf_op jit(solution)/shard_map/all_gather | solution.py:56
  121.0 1.9 gather_fusion.1
  122.9 0.0 copy-done
  122.9 1.3 fusion.36
  124.1 0.2 fusion.16
  124.4 0.2 select_reduce_fusion
  124.6 0.1 copy.22
  124.7 168.1 %pmax.14 = f32[512,8]{1,0:T(8,128)S(1)} all-reduce(f32[512,8]{1,0:T(8,128)S(1)} %copy.22), channel_id=1, replica_groups=mesh['group'=32,'tp'=16] {'group'}, use_global_device_ids=true, to_apply=%region_2.3 | all-reduce | flops 4096 | bytes 32768 | tf_op jit(solution)/shard_map/pmax | solution.py:74
  292.8 0.6 gather_fusion.2
  293.4 1.2 fusion.22
  294.6 0.0 reduce-scatter.11.cloned.1.call-update
  294.6 0.0 reduce-scatter.7.cloned.1.call-start
  294.7 2.3 fusion.10
  297.0 0.0 copy-start.3
  297.0 0.0 copy-start.4
  297.0 0.0 copy-start.2
  297.0 2.4 fusion.13
  299.4 0.0 reduce-scatter.7.cloned.1.call-update
  299.5 0.0 reduce-scatter.9.cloned.1.call-start
  299.5 0.0 copy-done.3
  299.6 0.0 copy-done.4
  299.6 0.0 copy-done.2
  299.6 0.1 fusion.28
  299.8 0.2 dynamic_update_slice.9
  300.0 43.1 %pmax.15 = f32[16,32]{1,0:T(8,128)S(1)} all-reduce(f32[16,32]{1,0:T(8,128)S(1)} %dynamic_update_slice.9), channel_id=1, replica_groups=mesh['group'=32,'tp'=16] {'tp'}, use_global_device_ids=true, to_apply=%region_4.5 | all-reduce | flops 512 | bytes 4096 | tf_op jit(solution)/shard_map/pmax | solution.py:109
  343.1 61.4 %reduce-scatter.11.cloned.1.call-done = f32[16,8]{1,0:T(8,128)} async-done(((f32[512,8]{1,0:T(8,128)}), f32[16,8]{1,0:T(8,128)}) %reduce-scatter.11.cloned.1.call-update) | async-done | bytes 528 | tf_op jit(solution)/shard_map/reduce_scatter | solution.py:85
  404.5 0.8 add_multiply_fusion
  405.3 0.1 broadcast_multiply_fusion
  405.4 119.6 %reduce-scatter.7.cloned.1.call-done = f32[16,1024]{1,0:T(8,128)} async-done(((f32[512,1024]{1,0:T(8,128)}), f32[16,1024]{1,0:T(8,128)}) %reduce-scatter.7.cloned.1.call-update) | async-done | bytes 65552 | tf_op jit(solution)/shard_map/reduce_scatter | solution.py:84
  525.0 0.1 mul.150
  525.1 0.1 mul.140
  525.2 0.9 fusion.23
  526.1 0.0 copy-start.1
  526.1 0.7 copy-done.1
  526.7 0.0 reduce-scatter.9.cloned.1.call-update
  526.8 1.3 dynamic-slice.1
  528.7 0.2 dynamic_update_slice.11
  528.9 43.0 %all-reduce.1 = f32[16,32]{1,0:T(8,128)S(1)} all-reduce(f32[16,32]{1,0:T(8,128)S(1)} %dynamic_update_slice.11), channel_id=5, replica_groups=mesh['group'=32,'tp'=16] {'tp'}, use_global_device_ids=true, to_apply=%region_8.9.clone | all-reduce | flops 512 | bytes 4096
  571.9 0.1 constant_dynamic-slice_fusion.1
  572.0 40.6 %reduce-scatter.9.cloned.1.call-done = f32[16,256]{1,0:T(8,128)} async-done(((f32[16,4096]{1,0:T(8,128)}), f32[16,256]{1,0:T(8,128)}) %reduce-scatter.9.cloned.1.call-update) | async-done | bytes 16400 | tf_op jit(solution)/shard_map/reduce_scatter | solution.py:122
  612.6 0.1 div.32
  612.6 1.3 fusion.27
  (11 shorter events, 0.1 us)
Async XLA Ops:
  6.5 116.3 %copy-start = (bf16[1,64,1,128,128]{4,3,2,1,0:T(8,128)(2,1)S(1)}, bf16[1,64,1,128,128]{4,3,2,1,0:T(8,128)(2,1)}, u32[]{:S(2)}) copy-start(bf16[1,64,1,128,128]{4,3,2,1,0:T(8,128)(2,1)} %param.14) | copy-start | bytes 6291460
  6.5 114.5 %all-gather.2.cloned.1.call-start = ((), (), s32[]{:S(2)}) async-start(), calls=%async_computation.3 | async-start | bytes 1081344 | tf_op jit(solution)/shard_map/all_gather | solution.py:56
  52.0 352.5 %reduce-scatter.11.cloned.1.call-start = ((), (), s32[]{:S(2)}) async-start(), calls=%async_computation.6 | async-start | bytes 270336 | tf_op jit(solution)/shard_map/reduce_scatter | solution.py:85
  294.6 230.4 %reduce-scatter.7.cloned.1.call-start = ((), (), s32[]{:S(2)}) async-start(), calls=%async_computation.4 | async-start | bytes 2162688 | tf_op jit(solution)/shard_map/reduce_scatter | solution.py:84
  297.0 2.6 copy-start.3
  297.0 2.6 copy-start.4
  297.0 2.6 copy-start.2
  299.5 313.1 %reduce-scatter.9.cloned.1.call-start = ((), (), s32[]{:S(2)}) async-start(), calls=%async_computation.5 | async-start | bytes 278528 | tf_op jit(solution)/shard_map/reduce_scatter | solution.py:122
  526.1 0.7 copy-start.1
Sparse Core Ops, SparseCore 0:
  52.1 68.8 all-gather.1
  294.7 109.7 reduce-scatter.10
  408.9 116.0 reduce-scatter.6
  527.6 84.8 reduce-scatter.8
where the time goes:
time: 621 us; the launch traced here: 620 us
  blocking collectives  323 us (52%)
  waiting for transfers between devices  261 us (42%)
  between operations  14.7 us (2%)
  local copies, waits for them, and re-layouts  8.89 us (1%)
  matrix products  7.32 us (1%)
    pmax x1, blocking collectives, on_device(): global_top = lax.pmax(local_top, 'group')  168 us
    reduce_scatter x1, waiting for transfers between devices, on_device(): lax.psum_scatter(numer, 'group', scatter_dimension=0, tiled=True)  120 us
    unnamed x2, blocking collectives  66.9 us
    reduce_scatter x1, waiting for transfers between devices, on_device(): lax.psum_scatter(denom, 'group', scatter_dimension=0, tiled=True)  61.4 us
    all_gather x1, blocking collectives, on_device(): all_heads = lax.all_gather(queries, 'tp', axis=1, tiled=True)  44.8 us
    pmax x1, blocking collectives, on_device(): head_top = lax.pmax(wide_top, 'tp')  43.1 us
    reduce_scatter x1, waiting for transfers between devices, on_device(): lax.psum_scatter(wide_numer, 'tp', scatter_dimension=1, tiled=True)  40.6 us
    all_gather x1, waiting for transfers between devices, on_device(): lax.all_gather(own_queries, 'group', axis=0, tiled=True)  39.2 us
  transfers between devices with their start and end apart: 4, of which 4 were waited for; matrix products, arithmetic and copies ran while one was open for 2% of the time, Pallas kernels for 0%

commit v1 on v0

v1 whole, which is shorter than its diff:
```python
import functools

import jax
import jax.numpy as jnp
from jax import lax
from jax.experimental import pallas as pl
from jax.experimental.pallas import tpu as pltpu
from jax.sharding import PartitionSpec as P

QH = 32
KVH = 4
HD = 128
BLK = 512
SUB = 128
NZ = 4
NP = 8
NU = 4
NW = 4
ROWS = 16
PER = 2
SCALE = HD ** (-0.5)
LOW = -1e30
MESH = pl.DeviceIdType.MESH
F32 = jnp.float32
BF16 = jnp.bfloat16


def iota(shape, dim):
    return lax.broadcasted_iota(jnp.int32, shape, dim)


def kernel(
    q_ref, nk_ref, nv_ref, len_ref, row_ref, blk_ref, key_ref, value_ref, out_ref,
    kbuf, vbuf, qsend, qb, lsend, lb, tsend, tb, s2, qr, lr, osend, ssend, orecv, srecv, fos, fss, fo, fs,
    local_sem, send_sem, recv_sem, chunk_sem, chunk_len_sem,
):
    g = lax.axis_index("group")
    t = lax.axis_index("tp")
    z0, p0 = g // NP, lax.rem(g, NP)
    u, w = t // NW, lax.rem(t, NW)
    diagonal = u == w

    def place(zz, pp, uu, ww):
        return (zz * NP + pp, uu * NW + ww)

    key_copy = pltpu.make_async_copy(key_ref.at[0, :, 0], kbuf, local_sem.at[0])
    value_copy = pltpu.make_async_copy(value_ref.at[0, :, 0], vbuf, local_sem.at[1])
    key_copy.start()
    value_copy.start()

    barrier = pltpu.get_barrier_semaphore()

    def greet_far(d, carry):
        target = place(d // NW, p0, w, lax.rem(d, NW))

        @pl.when(jnp.logical_or(target[0] != g, target[1] != t))
        def _():
            pl.semaphore_signal(barrier, inc=1, device_id=target, device_id_type=MESH)

        return carry

    lax.fori_loop(0, NZ * NW, greet_far, 0)

    def greet_plane(d, carry):
        target = place(z0, d // NU, lax.rem(d, NU), w)

        @pl.when(jnp.logical_or(target[0] != g, target[1] != t))
        def _():
            pl.semaphore_signal(barrier, inc=1, device_id=target, device_id_type=MESH)

        return carry

    lax.fori_loop(0, NP * NU, greet_plane, 0)

    qsend[0:ROWS, :] = q_ref[:, 0:HD]
    qsend[ROWS : 2 * ROWS, :] = q_ref[:, HD : 2 * HD]
    lane1 = iota((1, HD), 1)
    lens = jnp.zeros((1, HD), jnp.int32)
    for r in range(ROWS):
        lens = jnp.where(lane1 == r, len_ref[r], lens)
    lsend[...] = lens
    for p in range(NP):
        row = jnp.zeros((1, HD), jnp.int32)
        for zz in range(NZ):
            for s in range(PER):
                row = jnp.where(
                    lane1 // 2 == p0 * 8 + zz * 2 + s, row_ref[0, (zz * NP + p) * PER + s], row
                )
        tsend[p] = row

    pl.semaphore_wait(barrier, NZ * NW + NP * NU - 1 - jnp.where(diagonal, 1, 0))

    def send(src, dst, target, which, recv):
        here = jnp.logical_and(target[0] == g, target[1] == t)

        @pl.when(jnp.logical_not(here))
        def _():
            pltpu.make_async_remote_copy(
                src_ref=src,
                dst_ref=dst,
                send_sem=send_sem.at[which],
                recv_sem=recv,
                device_id=target,
                device_id_type=MESH,
            ).start()

        @pl.when(here)
        def _():
            pltpu.make_async_copy(src, dst, recv).start()

    def a1(d, carry):
        zd, bd = d // NU, lax.rem(d, NU)
        send(qsend, qb.at[z0, pl.ds(pl.multiple_of(w * 32, 32), 32)], place(zd, p0, bd, u), 0, recv_sem.at[0])
        return carry

    lax.fori_loop(0, NZ * NU, a1, 0)

    def a1_lens(zd, carry):
        send(lsend, lb.at[z0], place(zd, p0, w, u), 1, recv_sem.at[1])
        return carry

    lax.fori_loop(0, NZ, a1_lens, 0)

    def table(pd, carry):
        send(tsend.at[pd], tb.at[p0], place(z0, pd, u, w), 2, recv_sem.at[2])
        return carry

    lax.fori_loop(0, NP, table, 0)
    pltpu.make_async_copy(tb, tb, recv_sem.at[2]).wait()

    rows = jnp.sum(tb[...], axis=0)
    sub = iota((HD, HD), 0)
    lane = iota((HD, HD), 1)
    head_match = lane // ROWS == 2 * (lax.rem(sub, 16) // 4) + lax.rem(sub, 2)
    lane_row = lax.rem(lane, ROWS)
    picks = []
    for zz in range(NZ):
        at = (sub // 16) * 16 + zz * 4 + lax.rem(sub, 4)
        wanted = jnp.sum(jnp.where(lane == at, rows, 0), axis=1, keepdims=True)
        picks.append(jnp.where(jnp.logical_and(head_match, lane_row == wanted), 1.0, 0.0).astype(BF16))

    nk = nk_ref[...].astype(F32)
    nv = nv_ref[...].astype(F32)
    fresh_key = jnp.zeros((ROWS, HD), F32)
    fresh_value = jnp.zeros((ROWS, HD), F32)
    for k in range(KVH):
        fresh_key = jnp.where(u == k, nk[:, k, :], fresh_key)
        fresh_value = jnp.where(u == k, nv[:, k, :], fresh_value)
    fresh_key = jnp.concatenate([fresh_key, fresh_key], axis=0)
    fresh_value = jnp.concatenate([fresh_value, fresh_value], axis=0)
    new_score = jnp.sum(qsend[...].astype(F32) * fresh_key, axis=1, keepdims=True) * SCALE

    pltpu.make_async_copy(qb, qb, recv_sem.at[0]).wait()
    pltpu.make_async_copy(lb, lb, recv_sem.at[1]).wait()
    for zz in range(NZ):
        chosen = jnp.dot(picks[zz], qb[zz], preferred_element_type=F32).astype(BF16)
        s2[:, zz] = chosen.reshape(NP, 16, HD)

    def a2(d, carry):
        pd = lax.rem(p0 + d, NP)
        send(s2.at[pd], qr.at[p0], place(z0, pd, u, w), 3, chunk_sem.at[p0])
        send(lb, lr.at[p0], place(z0, pd, u, w), 4, chunk_len_sem.at[p0])
        return carry

    lax.fori_loop(0, NP, a2, 0)
    key_copy.wait()
    value_copy.wait()

    row16 = iota((16, 2 * SUB), 0)
    lane2 = iota((16, 2 * SUB), 1)
    second = lax.rem(row16, 4) // 2
    token = jnp.where(second == lane2 // SUB, lax.rem(lane2, SUB), 1 << 20)
    second_col = lax.rem(iota((16, 1), 0), 4) // 2
    spot = iota((16, HD), 1) - p0 * 16 - lax.rem(iota((16, HD), 0), 4)

    def chunk(d, carry):
        p = lax.rem(p0 + d, NP)
        pltpu.make_async_copy(qr.at[p], qr.at[p], chunk_sem.at[p]).wait()
        pltpu.make_async_copy(lr.at[p], lr.at[p], chunk_len_sem.at[p]).wait()
        outs = []
        place_max = jnp.zeros((16, HD), F32)
        place_sum = jnp.zeros((16, HD), F32)
        for zz in range(NZ):
            slot = (zz * NP + p) * PER
            keys = kbuf[pl.ds(slot, PER)].reshape(PER * SUB, HD)
            values = vbuf[pl.ds(slot, PER)].reshape(PER * SUB, HD)
            score = (
                lax.dot_general(
                    qr[p, zz], keys, (((1,), (1,)), ((), ())), preferred_element_type=F32
                )
                * SCALE
            )
            live = []
            for s in range(PER):
                length = jnp.sum(
                    jnp.where(lane1 == row_ref[0, slot + s], lr[p, zz], 0), axis=1, keepdims=True
                )
                live.append(length - (blk_ref[0, slot + s] * BLK + u * SUB))
            valid = token < jnp.where(second_col == 0, live[0], live[1])
            masked = jnp.where(valid, score, LOW)
            top = jnp.max(masked, axis=1, keepdims=True)
            prob = jnp.where(valid, jnp.exp(masked - top), 0.0)
            total = jnp.sum(prob, axis=1, keepdims=True)
            outs.append(jnp.dot(prob.astype(BF16), values, preferred_element_type=F32))
            place_max = jnp.where(spot == zz * 4, top, place_max)
            place_sum = jnp.where(spot == zz * 4, total, place_sum)
        for j in range(NU):
            part = slice(4 * j, 4 * j + 4)
            osend[p, j] = jnp.concatenate([o[part] for o in outs], axis=0)
            ssend[p, j] = jnp.concatenate(
                [
                    jnp.sum(place_max[part], axis=0, keepdims=True),
                    jnp.sum(place_sum[part], axis=0, keepdims=True),
                ],
                axis=0,
            )

        def b1(j, inner):
            target = place(z0, p, j, w)
            send(osend.at[p, j], orecv.at[u * NP + p0], target, 5, recv_sem.at[3])
            send(ssend.at[p, j], srecv.at[u * NP + p0], target, 6, recv_sem.at[4])
            return inner

        lax.fori_loop(0, NU, b1, 0)
        return carry

    lax.fori_loop(0, NP, chunk, 0)

    match = jnp.logical_and(
        sub // 32 == lax.rem(lane, 16) // 4,
        jnp.logical_and(lax.rem(sub // 16, 2) == lax.rem(lane, 2), lax.rem(sub, 16) == rows),
    )
    pltpu.make_async_copy(srecv, srecv, recv_sem.at[4]).wait()
    tops, totals = [], []
    for b in range(NU):
        stats = jnp.sum(srecv[b * NP : (b + 1) * NP], axis=0)
        tops.append(jnp.where(match, stats[0:1], LOW))
        totals.append(stats[1:2])
    plane_top = jnp.max(
        jnp.maximum(jnp.maximum(tops[0], tops[1]), jnp.maximum(tops[2], tops[3])), axis=1, keepdims=True
    )
    weights = [jnp.where(match, jnp.exp(m - plane_top), 0.0) for m in tops]
    plane_sum = jnp.sum(sum(x * y for x, y in zip(weights, totals)), axis=1, keepdims=True)
    pltpu.make_async_copy(orecv, orecv, recv_sem.at[3]).wait()
    plane_out = jnp.zeros((HD, HD), F32)
    for b in range(NU):
        plane_out += jnp.dot(
            weights[b],
            orecv[b * NP : (b + 1) * NP].reshape(NP * 16, HD),
            precision=lax.Precision.HIGHEST,
            preferred_element_type=F32,
        )
    fos[...] = plane_out.reshape(NZ, 32, HD)
    packed = jnp.where(lane == lax.rem(sub, 32), plane_top, 0.0)
    packed = jnp.where(lane == 32 + lax.rem(sub, 32), plane_sum, packed)
    fss[...] = jnp.sum(packed.reshape(NZ, 32, HD), axis=1, keepdims=True)

    def b2(zd, carry):
        target = place(zd, p0, w, u)
        send(fos.at[zd], fo.at[z0], target, 7, recv_sem.at[5])
        send(fss.at[zd], fs.at[z0], target, 8, recv_sem.at[6])
        return carry

    lax.fori_loop(0, NZ, b2, 0)

    sub32 = iota((32, HD), 0)
    lane32 = iota((32, HD), 1)
    pltpu.make_async_copy(fs, fs, recv_sem.at[6]).wait()
    part_tops, part_sums = [], []
    for zz in range(NZ):
        part_tops.append(jnp.sum(jnp.where(lane32 == sub32, fs[zz], 0.0), axis=1, keepdims=True))
        part_sums.append(jnp.sum(jnp.where(lane32 == 32 + sub32, fs[zz], 0.0), axis=1, keepdims=True))
    last_top = new_score
    for m in part_tops:
        last_top = jnp.maximum(last_top, m)
    fresh = jnp.exp(new_score - last_top)
    denom = fresh
    numer = fresh * fresh_value
    factors = [jnp.exp(m - last_top) for m in part_tops]
    for zz in range(NZ):
        denom += factors[zz] * part_sums[zz]
    pltpu.make_async_copy(fo, fo, recv_sem.at[5]).wait()
    for zz in range(NZ):
        numer += factors[zz] * fo[zz]
    result = (numer / denom).astype(BF16)
    out_ref[:, 0:HD] = result[0:ROWS]
    out_ref[:, HD : 2 * HD] = result[ROWS : 2 * ROWS]

    def sent(ref, which):
        pltpu.make_async_copy(ref, ref, send_sem.at[which]).wait()

    def sent_unless_diagonal(ref, which):
        @pl.when(jnp.logical_not(diagonal))
        def _():
            sent(ref, which)

    blocks = qb.at[pl.ds(0, 3)]
    sent(blocks, 0)
    sent(qb.at[3, pl.ds(0, 96)], 0)
    sent_unless_diagonal(qsend, 0)
    sent(lb.at[pl.ds(0, 3)], 1)
    sent_unless_diagonal(lsend, 1)
    sent(tb.at[pl.ds(0, NP - 1)], 2)
    sent(qr.at[pl.ds(0, NP - 1)], 3)
    sent(lr.at[pl.ds(0, NP - 1)], 4)
    sent(orecv.at[pl.ds(0, NP * NU - 1)], 5)
    sent(srecv.at[pl.ds(0, NP * NU - 1)], 6)
    sent(fo.at[pl.ds(0, NZ - 1)], 7)
    sent_unless_diagonal(fo.at[0], 7)
    sent(fs.at[pl.ds(0, NZ - 1)], 8)
    sent_unless_diagonal(fs.at[0], 8)


def on_device(queries, new_key, new_value, lengths, slot_row, slot_block, key_cache, value_cache):
    vmem = pl.BlockSpec(memory_space=pltpu.VMEM)
    smem = pl.BlockSpec(memory_space=pltpu.SMEM)
    anywhere = pl.BlockSpec(memory_space=pl.ANY)
    slots = NZ * NP * PER
    return pl.pallas_call(
        kernel,
        out_shape=jax.ShapeDtypeStruct((ROWS, 2 * HD), BF16),
        in_specs=[vmem, vmem, vmem, smem, smem, smem, anywhere, anywhere],
        out_specs=vmem,
        scratch_shapes=[
            pltpu.VMEM((slots, SUB, HD), BF16),
            pltpu.VMEM((slots, SUB, HD), BF16),
            pltpu.VMEM((2 * ROWS, HD), BF16),
            pltpu.VMEM((NZ, HD, HD), BF16),
            pltpu.VMEM((1, HD), jnp.int32),
            pltpu.VMEM((NZ, 1, HD), jnp.int32),
            pltpu.VMEM((NP, 1, HD), jnp.int32),
            pltpu.VMEM((NP, 1, HD), jnp.int32),
            pltpu.VMEM((NP, NZ, 16, HD), BF16),
            pltpu.VMEM((NP, NZ, 16, HD), BF16),
            pltpu.VMEM((NP, NZ, 1, HD), jnp.int32),
            pltpu.VMEM((NP, NU, 16, HD), F32),
            pltpu.VMEM((NP, NU, 2, HD), F32),
            pltpu.VMEM((NU * NP, 16, HD), F32),
            pltpu.VMEM((NU * NP, 2, HD), F32),
            pltpu.VMEM((NZ, 32, HD), F32),
            pltpu.VMEM((NZ, 1, HD), F32),
            pltpu.VMEM((NZ, 32, HD), F32),
            pltpu.VMEM((NZ, 1, HD), F32),
            pltpu.SemaphoreType.DMA((2,)),
            pltpu.SemaphoreType.DMA((9,)),
            pltpu.SemaphoreType.DMA((7,)),
            pltpu.SemaphoreType.DMA((NP,)),
            pltpu.SemaphoreType.DMA((NP,)),
        ],
        compiler_params=pltpu.CompilerParams(
            collective_id=0, has_side_effects=True, vmem_limit_bytes=32 * 1024 * 1024
        ),
        cost_estimate=pl.CostEstimate(flops=2 * 2 * 2 * 8 * slots * SUB * HD, bytes_accessed=2 * slots * SUB * HD * 2, transcendentals=slots * 16 * SUB),
    )(queries, new_key, new_value, lengths, slot_row, slot_block, key_cache, value_cache)


def solution(mesh):
    in_specs = (
        P("group", "tp"),
        P("group", None, None),
        P("group", None, None),
        P("group"),
        P("group", None),
        P("group", None),
        P("group", None, "tp", None, None),
        P("group", None, "tp", None, None),
    )
    return jax.shard_map(
        on_device, mesh=mesh, in_specs=in_specs, out_specs=P("group", "tp"), check_vma=False
    )
```

time: 621 us -> 59.7 us (0.10)
  the two profiles are of different devices: /device:TPU:6 before, /device:TPU:27 now
where the time goes in v1:
time: 59.7 us; the launch traced here: 59.4 us
  Pallas kernels  51.5 us (86%)
  local copies, waits for them, and re-layouts  7.88 us (13%)
    pallas_call x1, Pallas kernels, on_device(): pl.pallas_call(kernel, out_shape=jax.ShapeDtypeStruct((ROWS, 2 * HD), BF1...  51.5 us
    unnamed x17, local copies, waits for them, and re-layouts  7.88 us

profile of v1, /device:TPU:27, one launch (start us, length us, event | category | flops | bytes accessed | tf_op | source)
XLA Modules:
  0.0 59.4 jit_solution(15971315150767354840)
XLA Ops:
  0.0 0.0 copy-start
  0.0 1.6 %copy-done = bf16[1,64,1,128,128]{4,3,2,1,0:T(8,128)(2,1)S(1)} copy-done((bf16[1,64,1,128,128]{4,3,2,1,0:T(8,128)(2,1)S(1)}, bf16[1,64,1,128,128]{4,3,2,1,0:T(8,128)(2,1)}, u32[]{:S(2)}) %copy-start) | copy-done | bytes 2097176
  1.6 0.0 copy-start.1
  1.6 1.6 %copy-done.1 = bf16[1,64,1,128,128]{4,3,2,1,0:T(8,128)(2,1)S(1)} copy-done((bf16[1,64,1,128,128]{4,3,2,1,0:T(8,128)(2,1)S(1)}, bf16[1,64,1,128,128]{4,3,2,1,0:T(8,128)(2,1)}, u32[]{:S(2)}) %copy-start.1) | copy-done | bytes 2097176
  3.2 0.0 copy-start.2
  3.2 0.7 %copy-done.2 = bf16[16,4,128]{2,1,0:T(4,128)(2,1)S(1)} copy-done((bf16[16,4,128]{2,1,0:T(4,128)(2,1)S(1)}, bf16[16,4,128]{2,1,0:T(4,128)(2,1)}, u32[]{:S(2)}) %copy-start.2) | copy-done | bytes 16408
  3.9 0.0 copy-start.3
  3.9 0.7 %copy-done.3 = bf16[16,4,128]{2,1,0:T(4,128)(2,1)S(1)} copy-done((bf16[16,4,128]{2,1,0:T(4,128)(2,1)S(1)}, bf16[16,4,128]{2,1,0:T(4,128)(2,1)}, u32[]{:S(2)}) %copy-start.3) | copy-done | bytes 16408
  4.6 0.0 copy-start.4
  4.6 0.7 %copy-done.4 = bf16[16,256]{1,0:T(8,128)(2,1)S(1)} copy-done((bf16[16,256]{1,0:T(8,128)(2,1)S(1)}, bf16[16,256]{1,0:T(8,128)(2,1)}, u32[]{:S(2)}) %copy-start.4) | copy-done | bytes 8216
  5.3 0.0 copy-start.5
  5.3 0.7 %copy-done.5 = s32[16]{0:T(128)S(1)} copy-done((s32[16]{0:T(128)S(1)}, s32[16]{0:T(128)}, u32[]{:S(2)}) %copy-start.5) | copy-done | bytes 88
  6.0 0.0 copy-start.6
  6.0 0.7 %copy-done.6 = s32[1,64]{1,0:T(1,128)S(1)} copy-done((s32[1,64]{1,0:T(1,128)S(1)}, s32[1,64]{1,0:T(1,128)}, u32[]{:S(2)}) %copy-start.6) | copy-done | bytes 280
  6.6 0.0 copy-start.7
  6.6 0.7 %copy-done.7 = s32[1,64]{1,0:T(1,128)S(1)} copy-done((s32[1,64]{1,0:T(1,128)S(1)}, s32[1,64]{1,0:T(1,128)}, u32[]{:S(2)}) %copy-start.7) | copy-done | bytes 280
  7.3 51.5 %shard_map.82 = bf16[16,256]{1,0:T(8,128)(2,1)S(1)} custom-call(bf16[16,256]{1,0:T(8,128)(2,1)S(1)} %copy-done.4, bf16[16,4,128]{2,1,0:T(4,128)(2,1)S(1)} %copy-done.2, bf16[16,4,128]{2,1,0:T(4,128)(2,1)S(1)} %copy-done.3, s32[16]{0:T(128)S(1)} %copy-done.5, s32[1,64]{1,0:T(1,128)S(1)} %copy-done.6, s32[1,64]{1,0:T(1,128)S(1)} %copy-done.7, ...), custom_call_target="tpu_custom_call" | custom-call | flops 67108864 | bytes 4194304 | tf_op jit(solution)/shard_map/pallas_call | solution.py:319
  58.8 0.6 %copy.10 = bf16[16,256]{1,0:T(8,128)(2,1)} copy(bf16[16,256]{1,0:T(8,128)(2,1)S(1)} %shard_map.82) | data formatting | bytes 16384
Async XLA Ops:
  0.0 1.6 %copy-start = (bf16[1,64,1,128,128]{4,3,2,1,0:T(8,128)(2,1)S(1)}, bf16[1,64,1,128,128]{4,3,2,1,0:T(8,128)(2,1)}, u32[]{:S(2)}) copy-start(bf16[1,64,1,128,128]{4,3,2,1,0:T(8,128)(2,1)} %key_ref.1) | copy-start | bytes 6291460
  1.6 1.6 %copy-start.1 = (bf16[1,64,1,128,128]{4,3,2,1,0:T(8,128)(2,1)S(1)}, bf16[1,64,1,128,128]{4,3,2,1,0:T(8,128)(2,1)}, u32[]{:S(2)}) copy-start(bf16[1,64,1,128,128]{4,3,2,1,0:T(8,128)(2,1)} %value_ref.1) | copy-start | bytes 6291460
  3.2 0.7 %copy-start.2 = (bf16[16,4,128]{2,1,0:T(4,128)(2,1)S(1)}, bf16[16,4,128]{2,1,0:T(4,128)(2,1)}, u32[]{:S(2)}) copy-start(bf16[16,4,128]{2,1,0:T(4,128)(2,1)} %nk_ref.1) | copy-start | bytes 49156
  3.9 0.7 %copy-start.3 = (bf16[16,4,128]{2,1,0:T(4,128)(2,1)S(1)}, bf16[16,4,128]{2,1,0:T(4,128)(2,1)}, u32[]{:S(2)}) copy-start(bf16[16,4,128]{2,1,0:T(4,128)(2,1)} %nv_ref.1) | copy-start | bytes 49156
  4.6 0.7 %copy-start.4 = (bf16[16,256]{1,0:T(8,128)(2,1)S(1)}, bf16[16,256]{1,0:T(8,128)(2,1)}, u32[]{:S(2)}) copy-start(bf16[16,256]{1,0:T(8,128)(2,1)} %q_ref.1) | copy-start | bytes 24580
  5.3 0.7 %copy-start.5 = (s32[16]{0:T(128)S(1)}, s32[16]{0:T(128)}, u32[]{:S(2)}) copy-start(s32[16]{0:T(128)} %len_ref.1) | copy-start | bytes 196
  6.0 0.7 %copy-start.6 = (s32[1,64]{1,0:T(1,128)S(1)}, s32[1,64]{1,0:T(1,128)}, u32[]{:S(2)}) copy-start(s32[1,64]{1,0:T(1,128)} %row_ref.1) | copy-start | bytes 772
  6.6 0.7 %copy-start.7 = (s32[1,64]{1,0:T(1,128)S(1)}, s32[1,64]{1,0:T(1,128)}, u32[]{:S(2)}) copy-start(s32[1,64]{1,0:T(1,128)} %blk_ref.1) | copy-start | bytes 772

commit v2 on v1

--- a/solution.py
+++ b/solution.py
@@ -30,9 +30,10 @@
 
 
 def kernel(
-    q_ref, nk_ref, nv_ref, len_ref, row_ref, blk_ref, key_ref, value_ref, out_ref,
-    kbuf, vbuf, qsend, qb, lsend, lb, tsend, tb, s2, qr, lr, osend, ssend, orecv, srecv, fos, fss, fo, fs,
-    local_sem, send_sem, recv_sem, chunk_sem, chunk_len_sem,
+    q_hbm, nk_hbm, nv_hbm, len_hbm, row_hbm, blk_hbm, key_hbm, value_hbm, out_ref,
+    q_ref, nk_ref, nv_ref, len_ref, row_ref, blk_ref, kbuf, vbuf,
+    qsend, qb, lsend, lb, tsend, tb, s2, qr, osend, ssend, orecv, srecv, fos, fss, fo, fs,
+    local_sem, send_sem, recv_sem, chunk_sem,
 ):
     g = lax.axis_index("group")
     t = lax.axis_index("tp")
@@ -43,34 +44,43 @@
     def place(zz, pp, uu, ww):
         return (zz * NP + pp, uu * NW + ww)
 
-    key_copy = pltpu.make_async_copy(key_ref.at[0, :, 0], kbuf, local_sem.at[0])
-    value_copy = pltpu.make_async_copy(value_ref.at[0, :, 0], vbuf, local_sem.at[1])
-    key_copy.start()
-    value_copy.start()
-
     barrier = pltpu.get_barrier_semaphore()
 
+    def greet(target):
+        pl.semaphore_signal(barrier, inc=1, device_id=target, device_id_type=MESH)
+
     def greet_far(d, carry):
-        target = place(d // NW, p0, w, lax.rem(d, NW))
+        target = place(lax.rem(z0 + 2 + d // NW, NZ), p0, w, lax.rem(d, NW))
 
         @pl.when(jnp.logical_or(target[0] != g, target[1] != t))
         def _():
-            pl.semaphore_signal(barrier, inc=1, device_id=target, device_id_type=MESH)
+            greet(target)
 
         return carry
 
     lax.fori_loop(0, NZ * NW, greet_far, 0)
+    small = [
+        pltpu.make_async_copy(src, dst, local_sem.at[i])
+        for i, (src, dst) in enumerate(
+            ((q_hbm, q_ref), (len_hbm, len_ref), (row_hbm, row_ref), (blk_hbm, blk_ref), (nk_hbm, nk_ref), (nv_hbm, nv_ref))
+        )
+    ]
+    key_copy = pltpu.make_async_copy(key_hbm.at[0, :, 0], kbuf, local_sem.at[6])
+    value_copy = pltpu.make_async_copy(value_hbm.at[0, :, 0], vbuf, local_sem.at[7])
+    for copy in small[:4]:
+        copy.start()
 
     def greet_plane(d, carry):
-        target = place(z0, d // NU, lax.rem(d, NU), w)
-
-        @pl.when(jnp.logical_or(target[0] != g, target[1] != t))
-        def _():
-            pl.semaphore_signal(barrier, inc=1, device_id=target, device_id_type=MESH)
-
-        return carry
-
-    lax.fori_loop(0, NP * NU, greet_plane, 0)
+        greet(place(z0, lax.rem(p0 + d, NP), u, w))
+        return carry
+
+    lax.fori_loop(1, NP, greet_plane, 0)
+    for d in range(1, NU):
+        greet(place(z0, p0, lax.rem(u + d, NU), w))
+    for copy in (*small[4:], key_copy, value_copy):
+        copy.start()
+    for copy in small[:4]:
+        copy.wait()
 
     qsend[0:ROWS, :] = q_ref[:, 0:HD]
     qsend[ROWS : 2 * ROWS, :] = q_ref[:, HD : 2 * HD]
@@ -88,7 +98,7 @@
                 )
         tsend[p] = row
 
-    pl.semaphore_wait(barrier, NZ * NW + NP * NU - 1 - jnp.where(diagonal, 1, 0))
+    pl.semaphore_wait(barrier, NZ * NW + NP - 1 + NU - 1 - jnp.where(diagonal, 1, 0))
 
     def send(src, dst, target, which, recv):
         here = jnp.logical_and(target[0] == g, target[1] == t)
@@ -109,7 +119,7 @@
             pltpu.make_async_copy(src, dst, recv).start()
 
     def a1(d, carry):
-        zd, bd = d // NU, lax.rem(d, NU)
+        zd, bd = lax.rem(z0 + 2 + d // NU, NZ), lax.rem(d, NU)
         send(qsend, qb.at[z0, pl.ds(pl.multiple_of(w * 32, 32), 32)], place(zd, p0, bd, u), 0, recv_sem.at[0])
         return carry
 
@@ -139,6 +149,8 @@
         wanted = jnp.sum(jnp.where(lane == at, rows, 0), axis=1, keepdims=True)
         picks.append(jnp.where(jnp.logical_and(head_match, lane_row == wanted), 1.0, 0.0).astype(BF16))
 
+    small[4].wait()
+    small[5].wait()
     nk = nk_ref[...].astype(F32)
     nv = nv_ref[...].astype(F32)
     fresh_key = jnp.zeros((ROWS, HD), F32)
@@ -154,56 +166,78 @@
     pltpu.make_async_copy(lb, lb, recv_sem.at[1]).wait()
     for zz in range(NZ):
         chosen = jnp.dot(picks[zz], qb[zz], preferred_element_type=F32).astype(BF16)
-        s2[:, zz] = chosen.reshape(NP, 16, HD)
+        s2[:, zz * 16 : zz * 16 + 16] = chosen.reshape(NP, 16, HD)
+    lens = jnp.concatenate([lb[zz] for zz in range(NZ)] + [jnp.zeros((16 - NZ, HD), jnp.int32)], axis=0)
+    low = pltpu.roll(lax.rem(lens, 128), 16, 1)
+    coded = jnp.where(iota((16, HD), 1) < ROWS, lens // 128, low).astype(F32).astype(BF16)
+    s2[:, NZ * 16 : NZ * 16 + 16] = jnp.broadcast_to(coded[None], (NP, 16, HD))
 
     def a2(d, carry):
         pd = lax.rem(p0 + d, NP)
         send(s2.at[pd], qr.at[p0], place(z0, pd, u, w), 3, chunk_sem.at[p0])
-        send(lb, lr.at[p0], place(z0, pd, u, w), 4, chunk_len_sem.at[p0])
         return carry
 
     lax.fori_loop(0, NP, a2, 0)
     key_copy.wait()
     value_copy.wait()
 
-    row16 = iota((16, 2 * SUB), 0)
-    lane2 = iota((16, 2 * SUB), 1)
-    second = lax.rem(row16, 4) // 2
+    row32 = iota((32, 2 * SUB), 0)
+    lane2 = iota((32, 2 * SUB), 1)
+    second = lax.rem(row32, 4) // 2
     token = jnp.where(second == lane2 // SUB, lax.rem(lane2, SUB), 1 << 20)
     second_col = lax.rem(iota((16, 1), 0), 4) // 2
     spot = iota((16, HD), 1) - p0 * 16 - lax.rem(iota((16, HD), 0), 4)
+    no_query = jnp.zeros((16, HD), BF16)
 
     def chunk(d, carry):
         p = lax.rem(p0 + d, NP)
         pltpu.make_async_copy(qr.at[p], qr.at[p], chunk_sem.at[p]).wait()
-        pltpu.make_async_copy(lr.at[p], lr.at[p], chunk_len_sem.at[p]).wait()
-        outs = []
-        place_max = jnp.zeros((16, HD), F32)
-        place_sum = jnp.zeros((16, HD), F32)
-        for zz in range(NZ):
+        coded = qr[p, NZ * 16 : NZ * 16 + 16].astype(F32)
+        outs, tops, totals = [], [], []
+
+        def limit(zz):
             slot = (zz * NP + p) * PER
-            keys = kbuf[pl.ds(slot, PER)].reshape(PER * SUB, HD)
-            values = vbuf[pl.ds(slot, PER)].reshape(PER * SUB, HD)
+            live = []
+            for s in range(PER):
+                row = row_ref[0, slot + s]
+                parts = jnp.where(lane1 == row, coded[zz : zz + 1] * 128.0, 0.0)
+                parts = jnp.where(lane1 == row + ROWS, coded[zz : zz + 1], parts)
+                length = jnp.sum(parts, axis=1, keepdims=True).astype(jnp.int32)
+                live.append(length - (blk_ref[0, slot + s] * BLK + u * SUB))
+            return jnp.where(second_col == 0, live[0], live[1])
+
+        def pair(ref, za, zb):
+            halves = [ref[pl.ds((zz * NP + p) * PER, PER)].reshape(PER * SUB, HD) for zz in (za, zb)]
+            return jnp.concatenate(halves, axis=1)
+
+        for za, zb in ((0, 1), (2, 3)):
+            query = jnp.concatenate(
+                [
+                    jnp.concatenate([qr[p, za * 16 : za * 16 + 16], no_query], axis=1),
+                    jnp.concatenate([no_query, qr[p, zb * 16 : zb * 16 + 16]], axis=1),
+                ],
+                axis=0,
+            )
             score = (
                 lax.dot_general(
-                    qr[p, zz], keys, (((1,), (1,)), ((), ())), preferred_element_type=F32
+                    query, pair(kbuf, za, zb), (((1,), (1,)), ((), ())), preferred_element_type=F32
                 )
                 * SCALE
             )
-            live = []
-            for s in range(PER):
-                length = jnp.sum(
-                    jnp.where(lane1 == row_ref[0, slot + s], lr[p, zz], 0), axis=1, keepdims=True
-                )
-                live.append(length - (blk_ref[0, slot + s] * BLK + u * SUB))
-            valid = token < jnp.where(second_col == 0, live[0], live[1])
+            valid = token < jnp.concatenate([limit(za), limit(zb)], axis=0)
             masked = jnp.where(valid, score, LOW)
             top = jnp.max(masked, axis=1, keepdims=True)
             prob = jnp.where(valid, jnp.exp(masked - top), 0.0)
             total = jnp.sum(prob, axis=1, keepdims=True)
-            outs.append(jnp.dot(prob.astype(BF16), values, preferred_element_type=F32))
-            place_max = jnp.where(spot == zz * 4, top, place_max)
-            place_sum = jnp.where(spot == zz * 4, total, place_sum)
+            both = jnp.dot(prob.astype(BF16), pair(vbuf, za, zb), preferred_element_type=F32)
+            outs += [both[:16, :HD], both[16:, HD:]]
+            tops += [top[:16], top[16:]]
+            totals += [total[:16], total[16:]]
+        place_max = jnp.zeros((16, HD), F32)
+        place_sum = jnp.zeros((16, HD), F32)
+        for zz in range(NZ):
+            place_max = jnp.where(spot == zz * 4, tops[zz], place_max)
+            place_sum = jnp.where(spot == zz * 4, totals[zz], place_sum)
         for j in range(NU):
             part = slice(4 * j, 4 * j + 4)
             osend[p, j] = jnp.concatenate([o[part] for o in outs], axis=0)
@@ -255,7 +289,8 @@
     packed = jnp.where(lane == 32 + lax.rem(sub, 32), plane_sum, packed)
     fss[...] = jnp.sum(packed.reshape(NZ, 32, HD), axis=1, keepdims=True)
 
-    def b2(zd, carry):
+    def b2(d, carry):
+        zd = lax.rem(z0 + 2 + d, NZ)
         target = place(zd, p0, w, u)
         send(fos.at[zd], fo.at[z0], target, 7, recv_sem.at[5])
         send(fss.at[zd], fs.at[z0], target, 8, recv_sem.at[6])
@@ -302,7 +337,6 @@
     sent_unless_diagonal(lsend, 1)
     sent(tb.at[pl.ds(0, NP - 1)], 2)
     sent(qr.at[pl.ds(0, NP - 1)], 3)
-    sent(lr.at[pl.ds(0, NP - 1)], 4)
     sent(orecv.at[pl.ds(0, NP * NU - 1)], 5)
     sent(srecv.at[pl.ds(0, NP * NU - 1)], 6)
     sent(fo.at[pl.ds(0, NZ - 1)], 7)
@@ -312,16 +346,20 @@
 
 
 def on_device(queries, new_key, new_value, lengths, slot_row, slot_block, key_cache, value_cache):
-    vmem = pl.BlockSpec(memory_space=pltpu.VMEM)
-    smem = pl.BlockSpec(memory_space=pltpu.SMEM)
-    anywhere = pl.BlockSpec(memory_space=pl.ANY)
+    hbm = pl.BlockSpec(memory_space=pltpu.HBM)
     slots = NZ * NP * PER
     return pl.pallas_call(
         kernel,
         out_shape=jax.ShapeDtypeStruct((ROWS, 2 * HD), BF16),
-        in_specs=[vmem, vmem, vmem, smem, smem, smem, anywhere, anywhere],
-        out_specs=vmem,
+        in_specs=[hbm] * 8,
+        out_specs=pl.BlockSpec(memory_space=pltpu.VMEM),
         scratch_shapes=[
+            pltpu.VMEM((ROWS, 2 * HD), BF16),
+            pltpu.VMEM((ROWS, KVH, HD), BF16),
+            pltpu.VMEM((ROWS, KVH, HD), BF16),
+            pltpu.SMEM((ROWS,), jnp.int32),
+            pltpu.SMEM((1, slots), jnp.int32),
+            pltpu.SMEM((1, slots), jnp.int32),
             pltpu.VMEM((slots, SUB, HD), BF16),
             pltpu.VMEM((slots, SUB, HD), BF16),
             pltpu.VMEM((2 * ROWS, HD), BF16),
@@ -330,9 +368,8 @@
             pltpu.VMEM((NZ, 1, HD), jnp.int32),
             pltpu.VMEM((NP, 1, HD), jnp.int32),
             pltpu.VMEM((NP, 1, HD), jnp.int32),
-            pltpu.VMEM((NP, NZ, 16, HD), BF16),
-            pltpu.VMEM((NP, NZ, 16, HD), BF16),
-            pltpu.VMEM((NP, NZ, 1, HD), jnp.int32),
+            pltpu.VMEM((NP, NZ * 16 + 16, HD), BF16),
+            pltpu.VMEM((NP, NZ * 16 + 16, HD), BF16),
             pltpu.VMEM((NP, NU, 16, HD), F32),
             pltpu.VMEM((NP, NU, 2, HD), F32),
             pltpu.VMEM((NU * NP, 16, HD), F32),
@@ -341,14 +378,13 @@
             pltpu.VMEM((NZ, 1, HD), F32),
             pltpu.VMEM((NZ, 32, HD), F32),
             pltpu.VMEM((NZ, 1, HD), F32),
-            pltpu.SemaphoreType.DMA((2,)),
+            pltpu.SemaphoreType.DMA((8,)),
             pltpu.SemaphoreType.DMA((9,)),
             pltpu.SemaphoreType.DMA((7,)),
             pltpu.SemaphoreType.DMA((NP,)),
-            pltpu.SemaphoreType.DMA((NP,)),
         ],
         compiler_params=pltpu.CompilerParams(
-            collective_id=0, has_side_effects=True, vmem_limit_bytes=32 * 1024 * 1024
+            collective_id=0, has_side_effects=True, vmem_limit_bytes=60 * 1024 * 1024
         ),
         cost_estimate=pl.CostEstimate(flops=2 * 2 * 2 * 8 * slots * SUB * HD, bytes_accessed=2 * slots * SUB * HD * 2, transcendentals=slots * 16 * SUB),
     )(queries, new_key, new_value, lengths, slot_row, slot_block, key_cache, value_cache)

time: 59.7 us -> 51.2 us (0.86)
  the two profiles are of different devices: /device:TPU:27 before, /device:TPU:34 now
where the time goes in v2:
time: 51.2 us; the launch traced here: 50.9 us
  Pallas kernels  49.6 us (97%)
  local copies, waits for them, and re-layouts  1.3 us (3%)
    pallas_call x1, Pallas kernels, on_device(): pl.pallas_call(kernel, out_shape=jax.ShapeDtypeStruct((ROWS, 2 * HD), BF1...  49.6 us
    unnamed x1, local copies, waits for them, and re-layouts  1.3 us

profile of v2, /device:TPU:34, one launch (start us, length us, event | category | flops | bytes accessed | tf_op | source)
XLA Modules:
  0.0 50.9 jit_solution(1526208342479453853)
XLA Ops:
  0.0 49.6 %shard_map.82 = bf16[16,256]{1,0:T(8,128)(2,1)} custom-call(bf16[16,256]{1,0:T(8,128)(2,1)} %q_hbm.1, bf16[16,4,128]{2,1,0:T(4,128)(2,1)} %nk_hbm.1, bf16[16,4,128]{2,1,0:T(4,128)(2,1)} %nv_hbm.1, s32[16]{0:T(128)} %len_hbm.1, s32[1,64]{1,0:T(1,128)} %row_hbm.1, s32[1,64]{1,0:T(1,128)} %blk_hbm.1, bf16[1,64,1,128,128]{4,3,2,1,0:T(8,128)(2,1)} %key_hbm.1, ...), custom_call_target="tpu_custom_call" | custom-call | flops 67108864 | bytes 4194304 | tf_op jit(solution)/shard_map/pallas_call | solution.py:351
  49.6 1.3 %copy.10 = bf16[16,256]{1,0:T(8,128)(2,1)} copy(bf16[16,256]{1,0:T(8,128)(2,1)} %shard_map.82) | data formatting | bytes 16384

commit v3 on v2

v3 whole, which is shorter than its diff:
```python
import functools

import jax
import jax.numpy as jnp
from jax import lax
from jax.experimental import pallas as pl
from jax.experimental.pallas import tpu as pltpu
from jax.sharding import PartitionSpec as P

QH = 32
KVH = 4
HD = 128
BLK = 512
SUB = 128
NZ = 4
NP = 8
NU = 4
NW = 4
ROWS = 16
PER = 2
FIRST = (0,)
REST = (1, 2, 3)
SCALE = HD ** (-0.5)
LOW = -1e30
MESH = pl.DeviceIdType.MESH
F32 = jnp.float32
BF16 = jnp.bfloat16


def iota(shape, dim):
    return lax.broadcasted_iota(jnp.int32, shape, dim)


def kernel(
    q_hbm, nk_hbm, nv_hbm, len_hbm, row_hbm, blk_hbm, key_hbm, value_hbm, out_ref,
    q_ref, nk_ref, nv_ref, len_ref, row_ref, blk_ref, kbuf, vbuf,
    qsend, qb, tsend, tb, qs, ls, qr, lr, first_o, rest_o, first_r, rest_r, fos, fss, fo, fs,
    local_sem, send_sem, recv_sem, chunk_sem, chunk_len_sem,
):
    g = lax.axis_index("group")
    t = lax.axis_index("tp")
    z0, p0 = g // NP, lax.rem(g, NP)
    u, w = t // NW, lax.rem(t, NW)
    diagonal = u == w

    def place(zz, pp, uu, ww):
        return (zz * NP + pp, uu * NW + ww)

    barrier = pltpu.get_barrier_semaphore()

    def greet(target):
        pl.semaphore_signal(barrier, inc=1, device_id=target, device_id_type=MESH)

    for step in (2, 1, 3):
        greet(place(lax.rem(z0 + step, NZ), p0, w, u))

    @pl.when(jnp.logical_not(diagonal))
    def _():
        greet(place(z0, p0, w, u))

    small = [
        pltpu.make_async_copy(src, dst, local_sem.at[i])
        for i, (src, dst) in enumerate(
            ((q_hbm, q_ref), (len_hbm, len_ref), (row_hbm, row_ref), (blk_hbm, blk_ref), (nk_hbm, nk_ref), (nv_hbm, nv_ref))
        )
    ]
    key_copy = pltpu.make_async_copy(key_hbm.at[0, :, 0], kbuf, local_sem.at[6])
    value_copy = pltpu.make_async_copy(value_hbm.at[0, :, 0], vbuf, local_sem.at[7])
    for copy in small[:4]:
        copy.start()

    def greet_plane(d, carry):
        greet(place(z0, lax.rem(p0 + d, NP), u, w))
        return carry

    lax.fori_loop(1, NP, greet_plane, 0)
    for d in range(1, NU):
        greet(place(z0, p0, lax.rem(u + d, NU), w))
    for copy in (*small[4:], key_copy, value_copy):
        copy.start()
    for copy in small[:4]:
        copy.wait()

    qsend[0:ROWS, :] = q_ref[:, 0:HD]
    qsend[ROWS : 2 * ROWS, :] = q_ref[:, HD : 2 * HD]
    lane1 = iota((1, HD), 1)
    lens = jnp.zeros((1, HD), jnp.int32)
    for r in range(ROWS):
        lens = jnp.where(lane1 == r, len_ref[r] // 128, lens)
        lens = jnp.where(lane1 == ROWS + r, lax.rem(len_ref[r], 128), lens)
    qsend[2 * ROWS :, :] = jnp.broadcast_to(lens, (ROWS, HD)).astype(F32).astype(BF16)
    first_spot = jnp.where(lax.rem(lane1, 8) < 4, lax.rem(lane1, 64) // 2, -1)
    for p in range(NP):
        first_row = jnp.zeros((1, HD), jnp.int32)
        rest_row = jnp.zeros((1, HD), jnp.int32)
        for s in range(PER):
            first_row = jnp.where(first_spot == p0 * 4 + s, row_ref[0, p * PER + s], first_row)
            for i, zz in enumerate(REST):
                rest_row = jnp.where(
                    lane1 // 2 == p0 * 8 + i * 2 + s, row_ref[0, (zz * NP + p) * PER + s], rest_row
                )
        tsend[p] = jnp.concatenate([first_row, rest_row], axis=0)

    pl.semaphore_wait(barrier, NZ + NP - 1 + NU - 1 - jnp.where(diagonal, 1, 0))

    def send(src, dst, target, which, recv):
        here = jnp.logical_and(target[0] == g, target[1] == t)

        @pl.when(jnp.logical_not(here))
        def _():
            pltpu.make_async_remote_copy(
                src_ref=src,
                dst_ref=dst,
                send_sem=send_sem.at[which],
                recv_sem=recv,
                device_id=target,
                device_id_type=MESH,
            ).start()

        @pl.when(here)
        def _():
            pltpu.make_async_copy(src, dst, recv).start()

    for step in (2, 1, 3, 0):
        send(qsend, qb.at[z0], place(lax.rem(z0 + step, NZ), p0, w, u), 0, recv_sem.at[0])

    def table(pd, carry):
        send(tsend.at[pd], tb.at[p0], place(z0, pd, u, w), 1, recv_sem.at[1])
        return carry

    lax.fori_loop(0, NP, table, 0)
    pltpu.make_async_copy(tb, tb, recv_sem.at[1]).wait()

    rows = jnp.sum(tb[...], axis=0)
    first_rows, rest_rows = rows[0:1], rows[1:2]
    sub = iota((HD, HD), 0)
    lane = iota((HD, HD), 1)
    at = (sub // 16) * 8 + lax.rem(sub, 16)
    first_wanted = jnp.sum(jnp.where(lane == at, first_rows, 0), axis=1, keepdims=True)
    rest_wanted = jnp.sum(jnp.where(lane == sub - 4, rest_rows, 0), axis=1, keepdims=True)
    wanted = jnp.where(lax.rem(iota((HD, 1), 0), 16) < 4, first_wanted, rest_wanted)
    sub192 = iota((HD, NZ * 48), 0)
    at = (lax.rem(sub192, 16) // 4) * 48 + lax.rem(sub192, 2) * ROWS + wanted
    picks = jnp.where(iota((HD, NZ * 48), 1) == at, 1.0, 0.0).astype(BF16)

    small[4].wait()
    small[5].wait()
    nk = nk_ref[...].astype(F32)
    nv = nv_ref[...].astype(F32)
    fresh_key = jnp.zeros((ROWS, HD), F32)
    fresh_value = jnp.zeros((ROWS, HD), F32)
    for kv in range(KVH):
        fresh_key = jnp.where(u == kv, nk[:, kv, :], fresh_key)
        fresh_value = jnp.where(u == kv, nv[:, kv, :], fresh_value)
    fresh_key = jnp.concatenate([fresh_key, fresh_key], axis=0)
    fresh_value = jnp.concatenate([fresh_value, fresh_value], axis=0)
    new_score = jnp.sum(qsend[0 : 2 * ROWS].astype(F32) * fresh_key, axis=1, keepdims=True) * SCALE

    pltpu.make_async_copy(qb, qb, recv_sem.at[0]).wait()
    ls[...] = jnp.concatenate([qb[k][2 * ROWS :].astype(F32)[0:4] for k in range(NZ)], axis=0).astype(BF16)

    chosen = jnp.dot(picks, qb[...].reshape(NZ * 48, HD), preferred_element_type=F32).astype(BF16)
    qs[...] = chosen.reshape(NP, 16, HD)

    def a2(d, carry):
        pd = lax.rem(p0 + d, NP)
        for step in range(NU):
            ud = lax.rem(u + step, NU)
            send(qs.at[pd], qr.at[p0, u], place(z0, pd, ud, w), 3, chunk_sem.at[p0])
        send(ls, lr.at[p0], place(z0, pd, u, w), 2, chunk_len_sem.at[p0])
        return carry

    lax.fori_loop(0, NP, a2, 0)
    key_copy.wait()
    value_copy.wait()

    row32 = iota((32, 2 * SUB), 0)
    lane2 = iota((32, 2 * SUB), 1)
    second = lax.rem(row32, 4) // 2
    token = jnp.where(second == lane2 // SUB, lax.rem(lane2, SUB), 1 << 20)
    second_col = lax.rem(iota((16, 1), 0), 4) // 2
    row4 = lax.rem(iota((16, HD), 0), 4)
    rest_spot = iota((16, HD), 1) - p0 * 16 - row4
    first_spot = iota((16, HD), 1) - lax.rem(u, 2) * 64 - p0 * 8 - row4
    no_query = jnp.zeros((16, HD), BF16)

    def attend(units):
        def limit(unit):
            _, coded, slot = unit
            live = []
            for s in range(PER):
                row = row_ref[0, slot + s]
                parts = jnp.where(lane1 == row, coded * 128.0, 0.0)
                parts = jnp.where(lane1 == row + ROWS, coded, parts)
                length = jnp.sum(parts, axis=1, keepdims=True).astype(jnp.int32)
                live.append(length - (blk_ref[0, slot + s] * BLK + u * SUB))
            return jnp.where(second_col == 0, live[0], live[1])

        def both(ref, pair):
            halves = [ref[pl.ds(slot, PER)].reshape(PER * SUB, HD) for _, _, slot in pair]
            return jnp.concatenate(halves, axis=1)

        results = []
        for i in range(0, len(units), 2):
            pair = units[i : i + 2]
            query = jnp.concatenate(
                [
                    jnp.concatenate([pair[0][0], no_query], axis=1),
                    jnp.concatenate([no_query, pair[1][0]], axis=1),
                ],
                axis=0,
            )
            score = (
                lax.dot_general(
                    query, both(kbuf, pair), (((1,), (1,)), ((), ())), preferred_element_type=F32
                )
                * SCALE
            )
            valid = token < jnp.concatenate([limit(pair[0]), limit(pair[1])], axis=0)
            masked = jnp.where(valid, score, LOW)
            top = jnp.max(masked, axis=1, keepdims=True)
            prob = jnp.where(valid, jnp.exp(masked - top), 0.0)
            total = jnp.sum(prob, axis=1, keepdims=True)
            out = jnp.dot(prob.astype(BF16), both(vbuf, pair), preferred_element_type=F32)
            results.append((out[:16, :HD], top[:16], total[:16]))
            results.append((out[16:, HD:], top[16:], total[16:]))
        return results

    def b1(p, results, spot, dst, recv_ref, which, recv):
        place_max = jnp.zeros((16, HD), F32)
        place_sum = jnp.zeros((16, HD), F32)
        for i, (_, top, total) in enumerate(results):
            place_max = jnp.where(spot == i * 4, top, place_max)
            place_sum = jnp.where(spot == i * 4, total, place_sum)
        for j in range(NU):
            part = slice(4 * j, 4 * j + 4)
            dst[p, j] = jnp.concatenate(
                [r[0][part] for r in results]
                + [
                    jnp.sum(place_max[part], axis=0, keepdims=True),
                    jnp.sum(place_sum[part], axis=0, keepdims=True),
                    jnp.zeros((2, HD), F32),
                ],
                axis=0,
            )

        def one(d, carry):
            j = lax.rem(u + 2 + d, NU)
            send(dst.at[p, j], recv_ref.at[u * NP + p0], place(z0, p, j, w), which, recv)
            return carry

        lax.fori_loop(0, NU, one, 0)

    def units(p, places):
        held = [qr[p, j].astype(F32) for j in range(NU)]
        coded = lr[p].astype(F32)
        found = []
        for zz in places:
            query = jnp.concatenate([x[4 * zz : 4 * zz + 4] for x in held], axis=0).astype(BF16)
            found.append((query, coded[4 * zz : 4 * zz + 1], (zz * NP + p) * PER))
        return found

    def first_chunk(d, carry):
        ps = [lax.rem(p0 + NP - 4 * d - i, NP) for i in range(4)]
        wanted = []
        for p in ps:
            pltpu.make_async_copy(qr.at[p], qr.at[p], chunk_sem.at[p]).wait()
            pltpu.make_async_copy(lr.at[p], lr.at[p], chunk_len_sem.at[p]).wait()
            wanted += units(p, FIRST)
        for p, result in zip(ps, attend(wanted)):
            b1(p, [result], first_spot, first_o, first_r, 4, recv_sem.at[2])
        return carry

    lax.fori_loop(0, NP // 4, first_chunk, 0)

    def rest_chunk(d, carry):
        ps = [lax.rem(p0 + NP - 2 * d - i, NP) for i in range(2)]
        results = attend(units(ps[0], REST) + units(ps[1], REST))
        b1(ps[0], results[: len(REST)], rest_spot, rest_o, rest_r, 5, recv_sem.at[3])
        b1(ps[1], results[len(REST) :], rest_spot, rest_o, rest_r, 5, recv_sem.at[3])
        return carry

    lax.fori_loop(0, NP // 2, rest_chunk, 0)

    sub32 = iota((32, HD), 0)
    lane32 = iota((32, HD), 1)

    def combine(places, match, blocks, stat):
        tops, sums = [], []
        for x in blocks:
            stats = jnp.sum(x, axis=0)
            tops.append(jnp.where(match, stats[stat : stat + 1], LOW))
            sums.append(stats[stat + 1 : stat + 2])
        top = tops[0]
        for x in tops[1:]:
            top = jnp.maximum(top, x)
        top = jnp.max(top, axis=1, keepdims=True)
        weights = [jnp.where(match, jnp.exp(x - top), 0.0) for x in tops]
        total = jnp.sum(sum(x * y for x, y in zip(weights, sums)), axis=1, keepdims=True)
        weights = jnp.concatenate(weights, axis=1)
        high = weights.astype(BF16)
        low = (weights - high.astype(F32)).astype(BF16)
        weights = jnp.concatenate([high, low], axis=0)
        blocks = jnp.concatenate([x.reshape(HD, HD) for x in blocks], axis=0)
        high = blocks.astype(BF16)
        low = (blocks - high.astype(F32)).astype(BF16)
        blocks = jnp.concatenate([high, low], axis=1)
        both = jnp.dot(weights, blocks, preferred_element_type=F32)
        size = 32 * len(places)
        out = both[:size, :HD] + (both[:size, HD:] + both[size:, :HD])
        for i, zz in enumerate(places):
            part = slice(32 * i, 32 * i + 32)
            fos[zz] = out[part]
            packed = jnp.where(lane32 == sub32, top[part], 0.0)
            packed = jnp.where(lane32 == 32 + sub32, total[part], packed)
            fss[zz] = jnp.sum(packed, axis=0, keepdims=True)
            target = place(zz, p0, w, u)
            send(fos.at[zz], fo.at[z0], target, 6, recv_sem.at[4])
            send(fss.at[zz], fs.at[z0], target, 7, recv_sem.at[5])

    match = jnp.logical_and(
        lax.rem(lane32, 8) < 4,
        jnp.logical_and(sub32 // 16 == lax.rem(lane32, 2), lax.rem(sub32, 16) == first_rows),
    )
    pltpu.make_async_copy(first_r, first_r, recv_sem.at[2]).wait()
    combine(FIRST, match, [first_r[b * 2 * NP : (b + 1) * 2 * NP] for b in range(NU // 2)], 4)

    sub96 = iota((96, HD), 0)
    lane96 = iota((96, HD), 1)
    match = jnp.logical_and(
        sub96 // 32 == lax.rem(lane96, 16) // 4,
        jnp.logical_and(lax.rem(sub96 // 16, 2) == lax.rem(lane96, 2), lax.rem(sub96, 16) == rest_rows),
    )
    pltpu.make_async_copy(rest_r, rest_r, recv_sem.at[3]).wait()
    combine(REST, match, [rest_r[b * NP : (b + 1) * NP] for b in range(NU)], 12)

    pltpu.make_async_copy(fs, fs, recv_sem.at[5]).wait()
    part_tops, part_sums = [], []
    for k in range(NZ):
        part_tops.append(jnp.sum(jnp.where(lane32 == sub32, fs[k], 0.0), axis=1, keepdims=True))
        part_sums.append(jnp.sum(jnp.where(lane32 == 32 + sub32, fs[k], 0.0), axis=1, keepdims=True))
    last_top = new_score
    for m in part_tops:
        last_top = jnp.maximum(last_top, m)
    fresh = jnp.exp(new_score - last_top)
    denom = fresh
    numer = fresh * fresh_value
    factors = [jnp.exp(m - last_top) for m in part_tops]
    for k in range(NZ):
        denom += factors[k] * part_sums[k]
    pltpu.make_async_copy(fo, fo, recv_sem.at[4]).wait()
    for k in range(NZ):
        numer += factors[k] * fo[k]
    result = (numer / denom).astype(BF16)
    out_ref[:, 0:HD] = result[0:ROWS]
    out_ref[:, HD : 2 * HD] = result[ROWS : 2 * ROWS]

    def sent(ref, which):
        pltpu.make_async_copy(ref, ref, send_sem.at[which]).wait()

    def sent_unless_diagonal(ref, which):
        @pl.when(jnp.logical_not(diagonal))
        def _():
            sent(ref, which)

    sent(qb.at[pl.ds(0, NZ - 1)], 0)
    sent_unless_diagonal(qsend, 0)
    sent(tb.at[pl.ds(0, NP - 1)], 1)
    sent(lr.at[pl.ds(0, NP - 1)], 2)
    sent(qr.at[pl.ds(0, NP - 1)], 3)
    sent(qr.at[0, pl.ds(0, NU - 1)], 3)
    sent(first_r.at[pl.ds(0, NP * NU - 1)], 4)
    sent(rest_r.at[pl.ds(0, NP * NU - 1)], 5)
    sent(fo.at[pl.ds(0, NZ - 1)], 6)
    sent_unless_diagonal(fo.at[0], 6)
    sent(fs.at[pl.ds(0, NZ - 1)], 7)
    sent_unless_diagonal(fs.at[0], 7)


def on_device(queries, new_key, new_value, lengths, slot_row, slot_block, key_cache, value_cache):
    hbm = pl.BlockSpec(memory_space=pltpu.HBM)
    slots = NZ * NP * PER
    return pl.pallas_call(
        kernel,
        out_shape=jax.ShapeDtypeStruct((ROWS, 2 * HD), BF16),
        in_specs=[hbm] * 8,
        out_specs=pl.BlockSpec(memory_space=pltpu.VMEM),
        scratch_shapes=[
            pltpu.VMEM((ROWS, 2 * HD), BF16),
            pltpu.VMEM((ROWS, KVH, HD), BF16),
            pltpu.VMEM((ROWS, KVH, HD), BF16),
            pltpu.SMEM((ROWS,), jnp.int32),
            pltpu.SMEM((1, slots), jnp.int32),
            pltpu.SMEM((1, slots), jnp.int32),
            pltpu.VMEM((slots, SUB, HD), BF16),
            pltpu.VMEM((slots, SUB, HD), BF16),
            pltpu.VMEM((3 * ROWS, HD), BF16),
            pltpu.VMEM((NZ, 3 * ROWS, HD), BF16),
            pltpu.VMEM((NP, 2, HD), jnp.int32),
            pltpu.VMEM((NP, 2, HD), jnp.int32),
            pltpu.VMEM((NP, 16, HD), BF16),
            pltpu.VMEM((16, HD), BF16),
            pltpu.VMEM((NP, NU, 16, HD), BF16),
            pltpu.VMEM((NP, 16, HD), BF16),
            pltpu.VMEM((NP, NU, 8, HD), F32),
            pltpu.VMEM((NP, NU, 16, HD), F32),
            pltpu.VMEM((NU * NP, 8, HD), F32),
            pltpu.VMEM((NU * NP, 16, HD), F32),
            pltpu.VMEM((NZ, 32, HD), F32),
            pltpu.VMEM((NZ, 1, HD), F32),
            pltpu.VMEM((NZ, 32, HD), F32),
            pltpu.VMEM((NZ, 1, HD), F32),
            pltpu.SemaphoreType.DMA((8,)),
            pltpu.SemaphoreType.DMA((8,)),
            pltpu.SemaphoreType.DMA((6,)),
            pltpu.SemaphoreType.DMA((NP,)),
            pltpu.SemaphoreType.DMA((NP,)),
        ],
        compiler_params=pltpu.CompilerParams(
            collective_id=0, has_side_effects=True, vmem_limit_bytes=60 * 1024 * 1024
        ),
        cost_estimate=pl.CostEstimate(flops=2 * 2 * 2 * 8 * slots * SUB * HD, bytes_accessed=2 * slots * SUB * HD * 2, transcendentals=slots * 16 * SUB),
    )(queries, new_key, new_value, lengths, slot_row, slot_block, key_cache, value_cache)


def solution(mesh):
    in_specs = (
        P("group", "tp"),
        P("group", None, None),
        P("group", None, None),
        P("group"),
        P("group", None),
        P("group", None),
        P("group", None, "tp", None, None),
        P("group", None, "tp", None, None),
    )
    return jax.shard_map(
        on_device, mesh=mesh, in_specs=in_specs, out_specs=P("group", "tp"), check_vma=False
    )
```

time: 51.2 us -> 47 us (0.918)
  the two profiles are of different devices: /device:TPU:34 before, /device:TPU:224 now
where the time goes in v3:
time: 47 us; the launch traced here: 46.8 us
  Pallas kernels  45.5 us (97%)
  local copies, waits for them, and re-layouts  1.3 us (3%)
    pallas_call x1, Pallas kernels, on_device(): pl.pallas_call(kernel, out_shape=jax.ShapeDtypeStruct((ROWS, 2 * HD), BF1...  45.5 us
    unnamed x1, local copies, waits for them, and re-layouts  1.3 us

profile of v3, /device:TPU:224, one launch (start us, length us, event | category | flops | bytes accessed | tf_op | source)
XLA Modules:
  0.0 46.8 jit_solution(5442356047933572666)
XLA Ops:
  0.0 45.5 %shard_map.82 = bf16[16,256]{1,0:T(8,128)(2,1)} custom-call(bf16[16,256]{1,0:T(8,128)(2,1)} %q_hbm.1, bf16[16,4,128]{2,1,0:T(4,128)(2,1)} %nk_hbm.1, bf16[16,4,128]{2,1,0:T(4,128)(2,1)} %nv_hbm.1, s32[16]{0:T(128)} %len_hbm.1, s32[1,64]{1,0:T(1,128)} %row_hbm.1, s32[1,64]{1,0:T(1,128)} %blk_hbm.1, bf16[1,64,1,128,128]{4,3,2,1,0:T(8,128)(2,1)} %key_hbm.1, ...), custom_call_target="tpu_custom_call" | custom-call | flops 67108864 | bytes 4194304 | tf_op jit(solution)/shard_map/pallas_call | solution.py:383
  45.5 1.3 %copy.10 = bf16[16,256]{1,0:T(8,128)(2,1)} copy(bf16[16,256]{1,0:T(8,128)(2,1)} %shard_map.82) | data formatting | bytes 16384

commit v4 on v3

--- a/solution.py
+++ b/solution.py
@@ -34,7 +34,7 @@
 def kernel(
     q_hbm, nk_hbm, nv_hbm, len_hbm, row_hbm, blk_hbm, key_hbm, value_hbm, out_ref,
     q_ref, nk_ref, nv_ref, len_ref, row_ref, blk_ref, kbuf, vbuf,
-    qsend, qb, tsend, tb, qs, ls, qr, lr, first_o, rest_o, first_r, rest_r, fos, fss, fo, fs,
+    qsend, qb, lsend, lb, tsend, tb, qs, qr, lr, first_o, rest_o, first_r, rest_r, fos, fss, fo, fs,
     local_sem, send_sem, recv_sem, chunk_sem, chunk_len_sem,
 ):
     g = lax.axis_index("group")
@@ -81,14 +81,15 @@
     for copy in small[:4]:
         copy.wait()
 
+    first_r[:, 6:8] = jnp.zeros((NU * NP, 2, HD), F32)
+    rest_r[:, 14:16] = jnp.zeros((NU * NP, 2, HD), F32)
     qsend[0:ROWS, :] = q_ref[:, 0:HD]
     qsend[ROWS : 2 * ROWS, :] = q_ref[:, HD : 2 * HD]
     lane1 = iota((1, HD), 1)
     lens = jnp.zeros((1, HD), jnp.int32)
     for r in range(ROWS):
-        lens = jnp.where(lane1 == r, len_ref[r] // 128, lens)
-        lens = jnp.where(lane1 == ROWS + r, lax.rem(len_ref[r], 128), lens)
-    qsend[2 * ROWS :, :] = jnp.broadcast_to(lens, (ROWS, HD)).astype(F32).astype(BF16)
+        lens = jnp.where(lane1 == r, len_ref[r], lens)
+    lsend[...] = lens
     first_spot = jnp.where(lax.rem(lane1, 8) < 4, lax.rem(lane1, 64) // 2, -1)
     for p in range(NP):
         first_row = jnp.zeros((1, HD), jnp.int32)
@@ -103,32 +104,41 @@
 
     pl.semaphore_wait(barrier, NZ + NP - 1 + NU - 1 - jnp.where(diagonal, 1, 0))
 
-    def send(src, dst, target, which, recv):
-        here = jnp.logical_and(target[0] == g, target[1] == t)
-
+    def send_away(src, dst, target, which, recv):
+        pltpu.make_async_remote_copy(
+            src_ref=src,
+            dst_ref=dst,
+            send_sem=send_sem.at[which],
+            recv_sem=recv,
+            device_id=target,
+            device_id_type=MESH,
+        ).start()
+
+    def send(src, dst, target, which, recv, here):
         @pl.when(jnp.logical_not(here))
         def _():
-            pltpu.make_async_remote_copy(
-                src_ref=src,
-                dst_ref=dst,
-                send_sem=send_sem.at[which],
-                recv_sem=recv,
-                device_id=target,
-                device_id_type=MESH,
-            ).start()
+            send_away(src, dst, target, which, recv)
 
         @pl.when(here)
         def _():
             pltpu.make_async_copy(src, dst, recv).start()
 
     for step in (2, 1, 3, 0):
-        send(qsend, qb.at[z0], place(lax.rem(z0 + step, NZ), p0, w, u), 0, recv_sem.at[0])
-
-    def table(pd, carry):
-        send(tsend.at[pd], tb.at[p0], place(z0, pd, u, w), 1, recv_sem.at[1])
+        target = place(lax.rem(z0 + step, NZ), p0, w, u)
+        if step:
+            send_away(qsend, qb.at[z0], target, 0, recv_sem.at[0])
+            send_away(lsend, lb.at[z0], target, 8, recv_sem.at[6])
+        else:
+            send(qsend, qb.at[z0], target, 0, recv_sem.at[0], diagonal)
+            send(lsend, lb.at[z0], target, 8, recv_sem.at[6], diagonal)
+
+    def table(d, carry):
+        pd = lax.rem(p0 + d, NP)
+        send_away(tsend.at[pd], tb.at[p0], place(z0, pd, u, w), 1, recv_sem.at[1])
         return carry
 
-    lax.fori_loop(0, NP, table, 0)
+    lax.fori_loop(1, NP, table, 0)
+    pltpu.make_async_copy(tsend.at[p0], tb.at[p0], recv_sem.at[1]).start()
     pltpu.make_async_copy(tb, tb, recv_sem.at[1]).wait()
 
     rows = jnp.sum(tb[...], axis=0)
@@ -139,9 +149,8 @@
     first_wanted = jnp.sum(jnp.where(lane == at, first_rows, 0), axis=1, keepdims=True)
     rest_wanted = jnp.sum(jnp.where(lane == sub - 4, rest_rows, 0), axis=1, keepdims=True)
     wanted = jnp.where(lax.rem(iota((HD, 1), 0), 16) < 4, first_wanted, rest_wanted)
-    sub192 = iota((HD, NZ * 48), 0)
-    at = (lax.rem(sub192, 16) // 4) * 48 + lax.rem(sub192, 2) * ROWS + wanted
-    picks = jnp.where(iota((HD, NZ * 48), 1) == at, 1.0, 0.0).astype(BF16)
+    at = (lax.rem(sub, 16) // 4) * 32 + lax.rem(sub, 2) * ROWS + wanted
+    picks = jnp.where(lane == at, 1.0, 0.0).astype(BF16)
 
     small[4].wait()
     small[5].wait()
@@ -154,23 +163,26 @@
         fresh_value = jnp.where(u == kv, nv[:, kv, :], fresh_value)
     fresh_key = jnp.concatenate([fresh_key, fresh_key], axis=0)
     fresh_value = jnp.concatenate([fresh_value, fresh_value], axis=0)
-    new_score = jnp.sum(qsend[0 : 2 * ROWS].astype(F32) * fresh_key, axis=1, keepdims=True) * SCALE
+    new_score = jnp.sum(qsend[...].astype(F32) * fresh_key, axis=1, keepdims=True) * SCALE
 
     pltpu.make_async_copy(qb, qb, recv_sem.at[0]).wait()
-    ls[...] = jnp.concatenate([qb[k][2 * ROWS :].astype(F32)[0:4] for k in range(NZ)], axis=0).astype(BF16)
-
-    chosen = jnp.dot(picks, qb[...].reshape(NZ * 48, HD), preferred_element_type=F32).astype(BF16)
+    chosen = jnp.dot(picks, qb[...].reshape(HD, HD), preferred_element_type=F32).astype(BF16)
     qs[...] = chosen.reshape(NP, 16, HD)
+    pltpu.make_async_copy(lb, lb, recv_sem.at[6]).wait()
 
     def a2(d, carry):
         pd = lax.rem(p0 + d, NP)
         for step in range(NU):
             ud = lax.rem(u + step, NU)
-            send(qs.at[pd], qr.at[p0, u], place(z0, pd, ud, w), 3, chunk_sem.at[p0])
-        send(ls, lr.at[p0], place(z0, pd, u, w), 2, chunk_len_sem.at[p0])
+            send_away(qs.at[pd], qr.at[p0, u], place(z0, pd, ud, w), 3, chunk_sem.at[p0])
+        send_away(lb, lr.at[p0], place(z0, pd, u, w), 2, chunk_len_sem.at[p0])
         return carry
 
-    lax.fori_loop(0, NP, a2, 0)
+    for step in range(1, NU):
+        send_away(qs.at[p0], qr.at[p0, u], place(z0, p0, lax.rem(u + step, NU), w), 3, chunk_sem.at[p0])
+    lax.fori_loop(1, NP, a2, 0)
+    pltpu.make_async_copy(qs.at[p0], qr.at[p0, u], chunk_sem.at[p0]).start()
+    pltpu.make_async_copy(lb, lr.at[p0], chunk_len_sem.at[p0]).start()
     key_copy.wait()
     value_copy.wait()
 
@@ -186,13 +198,11 @@
 
     def attend(units):
         def limit(unit):
-            _, coded, slot = unit
+            _, lengths, slot = unit
             live = []
             for s in range(PER):
                 row = row_ref[0, slot + s]
-                parts = jnp.where(lane1 == row, coded * 128.0, 0.0)
-                parts = jnp.where(lane1 == row + ROWS, coded, parts)
-                length = jnp.sum(parts, axis=1, keepdims=True).astype(jnp.int32)
+                length = jnp.sum(jnp.where(lane1 == row, lengths, 0), axis=1, keepdims=True)
                 live.append(length - (blk_ref[0, slot + s] * BLK + u * SUB))
             return jnp.where(second_col == 0, live[0], live[1])
 
@@ -227,6 +237,7 @@
         return results
 
     def b1(p, results, spot, dst, recv_ref, which, recv):
+        used = pl.ds(0, 4 * len(results) + 2)
         place_max = jnp.zeros((16, HD), F32)
         place_sum = jnp.zeros((16, HD), F32)
         for i, (_, top, total) in enumerate(results):
@@ -244,20 +255,17 @@
                 axis=0,
             )
 
-        def one(d, carry):
-            j = lax.rem(u + 2 + d, NU)
-            send(dst.at[p, j], recv_ref.at[u * NP + p0], place(z0, p, j, w), which, recv)
-            return carry
-
-        lax.fori_loop(0, NU, one, 0)
+        for step in (2, 1, 3):
+            j = lax.rem(u + step, NU)
+            send_away(dst.at[p, j, used], recv_ref.at[u * NP + p0, used], place(z0, p, j, w), which, recv)
+        send(dst.at[p, u, used], recv_ref.at[u * NP + p0, used], place(z0, p, u, w), which, recv, p == p0)
 
     def units(p, places):
         held = [qr[p, j].astype(F32) for j in range(NU)]
-        coded = lr[p].astype(F32)
         found = []
         for zz in places:
             query = jnp.concatenate([x[4 * zz : 4 * zz + 4] for x in held], axis=0).astype(BF16)
-            found.append((query, coded[4 * zz : 4 * zz + 1], (zz * NP + p) * PER))
+            found.append((query, lr[p, zz], (zz * NP + p) * PER))
         return found
 
     def first_chunk(d, carry):
@@ -315,14 +323,16 @@
             packed = jnp.where(lane32 == 32 + sub32, total[part], packed)
             fss[zz] = jnp.sum(packed, axis=0, keepdims=True)
             target = place(zz, p0, w, u)
-            send(fos.at[zz], fo.at[z0], target, 6, recv_sem.at[4])
-            send(fss.at[zz], fs.at[z0], target, 7, recv_sem.at[5])
+            here = jnp.logical_and(diagonal, z0 == zz)
+            send(fss.at[zz], fs.at[z0], target, 7, recv_sem.at[5], here)
+            send(fos.at[zz], fo.at[z0], target, 6, recv_sem.at[4], here)
 
     match = jnp.logical_and(
         lax.rem(lane32, 8) < 4,
         jnp.logical_and(sub32 // 16 == lax.rem(lane32, 2), lax.rem(sub32, 16) == first_rows),
     )
-    pltpu.make_async_copy(first_r, first_r, recv_sem.at[2]).wait()
+    arrived = first_r.at[:, pl.ds(0, 6)]
+    pltpu.make_async_copy(arrived, arrived, recv_sem.at[2]).wait()
     combine(FIRST, match, [first_r[b * 2 * NP : (b + 1) * 2 * NP] for b in range(NU // 2)], 4)
 
     sub96 = iota((96, HD), 0)
@@ -331,7 +341,8 @@
         sub96 // 32 == lax.rem(lane96, 16) // 4,
         jnp.logical_and(lax.rem(sub96 // 16, 2) == lax.rem(lane96, 2), lax.rem(sub96, 16) == rest_rows),
     )
-    pltpu.make_async_copy(rest_r, rest_r, recv_sem.at[3]).wait()
+    arrived = rest_r.at[:, pl.ds(0, 14)]
+    pltpu.make_async_copy(arrived, arrived, recv_sem.at[3]).wait()
     combine(REST, match, [rest_r[b * NP : (b + 1) * NP] for b in range(NU)], 12)
 
     pltpu.make_async_copy(fs, fs, recv_sem.at[5]).wait()
@@ -365,12 +376,14 @@
 
     sent(qb.at[pl.ds(0, NZ - 1)], 0)
     sent_unless_diagonal(qsend, 0)
+    sent(lb.at[pl.ds(0, NZ - 1)], 8)
+    sent_unless_diagonal(lsend, 8)
     sent(tb.at[pl.ds(0, NP - 1)], 1)
     sent(lr.at[pl.ds(0, NP - 1)], 2)
     sent(qr.at[pl.ds(0, NP - 1)], 3)
     sent(qr.at[0, pl.ds(0, NU - 1)], 3)
-    sent(first_r.at[pl.ds(0, NP * NU - 1)], 4)
-    sent(rest_r.at[pl.ds(0, NP * NU - 1)], 5)
+    sent(first_r.at[pl.ds(0, NP * NU - 1), pl.ds(0, 6)], 4)
+    sent(rest_r.at[pl.ds(0, NP * NU - 1), pl.ds(0, 14)], 5)
     sent(fo.at[pl.ds(0, NZ - 1)], 6)
     sent_unless_diagonal(fo.at[0], 6)
     sent(fs.at[pl.ds(0, NZ - 1)], 7)
@@ -394,14 +407,15 @@
             pltpu.SMEM((1, slots), jnp.int32),
             pltpu.VMEM((slots, SUB, HD), BF16),
             pltpu.VMEM((slots, SUB, HD), BF16),
-            pltpu.VMEM((3 * ROWS, HD), BF16),
-            pltpu.VMEM((NZ, 3 * ROWS, HD), BF16),
+            pltpu.VMEM((2 * ROWS, HD), BF16),
+            pltpu.VMEM((NZ, 2 * ROWS, HD), BF16),
+            pltpu.VMEM((1, HD), jnp.int32),
+            pltpu.VMEM((NZ, 1, HD), jnp.int32),
             pltpu.VMEM((NP, 2, HD), jnp.int32),
             pltpu.VMEM((NP, 2, HD), jnp.int32),
             pltpu.VMEM((NP, 16, HD), BF16),
-            pltpu.VMEM((16, HD), BF16),
             pltpu.VMEM((NP, NU, 16, HD), BF16),
-            pltpu.VMEM((NP, 16, HD), BF16),
+            pltpu.VMEM((NP, NZ, 1, HD), jnp.int32),
             pltpu.VMEM((NP, NU, 8, HD), F32),
             pltpu.VMEM((NP, NU, 16, HD), F32),
             pltpu.VMEM((NU * NP, 8, HD), F32),
@@ -411,8 +425,8 @@
             pltpu.VMEM((NZ, 32, HD), F32),
             pltpu.VMEM((NZ, 1, HD), F32),
             pltpu.SemaphoreType.DMA((8,)),
-            pltpu.SemaphoreType.DMA((8,)),
-            pltpu.SemaphoreType.DMA((6,)),
+            pltpu.SemaphoreType.DMA((9,)),
+            pltpu.SemaphoreType.DMA((7,)),
             pltpu.SemaphoreType.DMA((NP,)),
             pltpu.SemaphoreType.DMA((NP,)),
         ],

time: 47 us -> 45.2 us (0.962)
  Pallas kernels: 45.5 us -> 43.6 us
    pallas_call x1, Pallas kernels: 45.5 us -> 43.6 us  [on_device(): pl.pallas_call(kernel, out_shape=jax.ShapeDtypeStruct((ROWS, 2 * HD), BF1...]
where the time goes in v4:
time: 45.2 us; the launch traced here: 44.9 us
  Pallas kernels  43.6 us (96%)
  local copies, waits for them, and re-layouts  1.3 us (3%)
    pallas_call x1, Pallas kernels, on_device(): pl.pallas_call(kernel, out_shape=jax.ShapeDtypeStruct((ROWS, 2 * HD), BF1...  43.6 us
    unnamed x1, local copies, waits for them, and re-layouts  1.3 us

profile of v4, /device:TPU:224, one launch (start us, length us, event | category | flops | bytes accessed | tf_op | source)
XLA Modules:
  0.0 44.9 jit_solution(8605164713339351727)
XLA Ops:
  0.0 43.6 %shard_map.82 = bf16[16,256]{1,0:T(8,128)(2,1)} custom-call(bf16[16,256]{1,0:T(8,128)(2,1)} %q_hbm.1, bf16[16,4,128]{2,1,0:T(4,128)(2,1)} %nk_hbm.1, bf16[16,4,128]{2,1,0:T(4,128)(2,1)} %nv_hbm.1, s32[16]{0:T(128)} %len_hbm.1, s32[1,64]{1,0:T(1,128)} %row_hbm.1, s32[1,64]{1,0:T(1,128)} %blk_hbm.1, bf16[1,64,1,128,128]{4,3,2,1,0:T(8,128)(2,1)} %key_hbm.1, ...), custom_call_target="tpu_custom_call" | custom-call | flops 67108864 | bytes 4194304 | tf_op jit(solution)/shard_map/pallas_call | solution.py:396
  43.6 1.3 %copy.10 = bf16[16,256]{1,0:T(8,128)(2,1)} copy(bf16[16,256]{1,0:T(8,128)(2,1)} %shard_map.82) | data formatting | bytes 16384

commit v5 on v4

--- a/solution.py
+++ b/solution.py
@@ -127,10 +127,11 @@
         target = place(lax.rem(z0 + step, NZ), p0, w, u)
         if step:
             send_away(qsend, qb.at[z0], target, 0, recv_sem.at[0])
-            send_away(lsend, lb.at[z0], target, 8, recv_sem.at[6])
         else:
             send(qsend, qb.at[z0], target, 0, recv_sem.at[0], diagonal)
-            send(lsend, lb.at[z0], target, 8, recv_sem.at[6], diagonal)
+    for step in (2, 1, 3):
+        send_away(lsend, lb.at[z0], place(lax.rem(z0 + step, NZ), p0, w, u), 8, recv_sem.at[6])
+    send(lsend, lb.at[z0], place(z0, p0, w, u), 8, recv_sem.at[6], diagonal)
 
     def table(d, carry):
         pd = lax.rem(p0 + d, NP)
@@ -172,13 +173,13 @@
 
     def a2(d, carry):
         pd = lax.rem(p0 + d, NP)
-        for step in range(NU):
+        for step in (2, 1, 3, 0):
             ud = lax.rem(u + step, NU)
             send_away(qs.at[pd], qr.at[p0, u], place(z0, pd, ud, w), 3, chunk_sem.at[p0])
         send_away(lb, lr.at[p0], place(z0, pd, u, w), 2, chunk_len_sem.at[p0])
         return carry
 
-    for step in range(1, NU):
+    for step in (2, 1, 3):
         send_away(qs.at[p0], qr.at[p0, u], place(z0, p0, lax.rem(u + step, NU), w), 3, chunk_sem.at[p0])
     lax.fori_loop(1, NP, a2, 0)
     pltpu.make_async_copy(qs.at[p0], qr.at[p0, u], chunk_sem.at[p0]).start()
@@ -269,7 +270,7 @@
         return found
 
     def first_chunk(d, carry):
-        ps = [lax.rem(p0 + NP - 4 * d - i, NP) for i in range(4)]
+        ps = [lax.rem(p0 + NP - 2 * d - i, NP) for i in range(2)]
         wanted = []
         for p in ps:
             pltpu.make_async_copy(qr.at[p], qr.at[p], chunk_sem.at[p]).wait()
@@ -279,7 +280,7 @@
             b1(p, [result], first_spot, first_o, first_r, 4, recv_sem.at[2])
         return carry
 
-    lax.fori_loop(0, NP // 4, first_chunk, 0)
+    lax.fori_loop(0, NP // 2, first_chunk, 0)
 
     def rest_chunk(d, carry):
         ps = [lax.rem(p0 + NP - 2 * d - i, NP) for i in range(2)]
@@ -293,26 +294,25 @@
     sub32 = iota((32, HD), 0)
     lane32 = iota((32, HD), 1)
 
-    def combine(places, match, blocks, stat):
-        tops, sums = [], []
-        for x in blocks:
-            stats = jnp.sum(x, axis=0)
-            tops.append(jnp.where(match, stats[stat : stat + 1], LOW))
-            sums.append(stats[stat + 1 : stat + 2])
+    def prepare(blocks, stat):
+        stats = [jnp.sum(x, axis=0)[stat : stat + 2] for x in blocks]
+        blocks = jnp.concatenate([x.reshape(HD, HD) for x in blocks], axis=0)
+        high = blocks.astype(BF16)
+        low = (blocks - high.astype(F32)).astype(BF16)
+        return stats, jnp.concatenate([high, low], axis=1)
+
+    def combine(places, match, stats, blocks):
+        tops = [jnp.where(match, x[0:1], LOW) for x in stats]
         top = tops[0]
         for x in tops[1:]:
             top = jnp.maximum(top, x)
         top = jnp.max(top, axis=1, keepdims=True)
         weights = [jnp.where(match, jnp.exp(x - top), 0.0) for x in tops]
-        total = jnp.sum(sum(x * y for x, y in zip(weights, sums)), axis=1, keepdims=True)
+        total = jnp.sum(sum(x * y[1:2] for x, y in zip(weights, stats)), axis=1, keepdims=True)
         weights = jnp.concatenate(weights, axis=1)
         high = weights.astype(BF16)
         low = (weights - high.astype(F32)).astype(BF16)
         weights = jnp.concatenate([high, low], axis=0)
-        blocks = jnp.concatenate([x.reshape(HD, HD) for x in blocks], axis=0)
-        high = blocks.astype(BF16)
-        low = (blocks - high.astype(F32)).astype(BF16)
-        blocks = jnp.concatenate([high, low], axis=1)
         both = jnp.dot(weights, blocks, preferred_element_type=F32)
         size = 32 * len(places)
         out = both[:size, :HD] + (both[:size, HD:] + both[size:, :HD])
@@ -333,7 +333,7 @@
     )
     arrived = first_r.at[:, pl.ds(0, 6)]
     pltpu.make_async_copy(arrived, arrived, recv_sem.at[2]).wait()
-    combine(FIRST, match, [first_r[b * 2 * NP : (b + 1) * 2 * NP] for b in range(NU // 2)], 4)
+    combine(FIRST, match, *prepare([first_r[b * 2 * NP : (b + 1) * 2 * NP] for b in range(NU // 2)], 4))
 
     sub96 = iota((96, HD), 0)
     lane96 = iota((96, HD), 1)
@@ -343,7 +343,9 @@
     )
     arrived = rest_r.at[:, pl.ds(0, 14)]
     pltpu.make_async_copy(arrived, arrived, recv_sem.at[3]).wait()
-    combine(REST, match, [rest_r[b * NP : (b + 1) * NP] for b in range(NU)], 12)
+    prepared = prepare([rest_r[b * NP : (b + 1) * NP] for b in range(NU)], 12)
+    combine(REST[:1], match[:32], *prepared)
+    combine(REST[1:], match[32:], *prepared)
 
     pltpu.make_async_copy(fs, fs, recv_sem.at[5]).wait()
     part_tops, part_sums = [], []

time: 45.2 us -> 44.8 us (level)
  no operation moved by 1% of the time
where the time goes in v5:
time: 44.8 us; the launch traced here: 44.6 us
  Pallas kernels  43.3 us (97%)
  local copies, waits for them, and re-layouts  1.3 us (3%)
    pallas_call x1, Pallas kernels, on_device(): pl.pallas_call(kernel, out_shape=jax.ShapeDtypeStruct((ROWS, 2 * HD), BF1...  43.3 us
    unnamed x1, local copies, waits for them, and re-layouts  1.3 us

profile of v5, /device:TPU:224, one launch (start us, length us, event | category | flops | bytes accessed | tf_op | source)
XLA Modules:
  0.0 44.6 jit_solution(957499574294137647)
XLA Ops:
  0.0 43.3 %shard_map.82 = bf16[16,256]{1,0:T(8,128)(2,1)} custom-call(bf16[16,256]{1,0:T(8,128)(2,1)} %q_hbm.1, bf16[16,4,128]{2,1,0:T(4,128)(2,1)} %nk_hbm.1, bf16[16,4,128]{2,1,0:T(4,128)(2,1)} %nv_hbm.1, s32[16]{0:T(128)} %len_hbm.1, s32[1,64]{1,0:T(1,128)} %row_hbm.1, s32[1,64]{1,0:T(1,128)} %blk_hbm.1, bf16[1,64,1,128,128]{4,3,2,1,0:T(8,128)(2,1)} %key_hbm.1, ...), custom_call_target="tpu_custom_call" | custom-call | flops 67108864 | bytes 4194304 | tf_op jit(solution)/shard_map/pallas_call | solution.py:398
  43.3 1.3 %copy.10 = bf16[16,256]{1,0:T(8,128)(2,1)} copy(bf16[16,256]{1,0:T(8,128)(2,1)} %shard_map.82) | data formatting | bytes 16384
